TPU v7x, 128 devices: a whole 4x4x4 slice. The times are simulated.
128 devices in a mesh: sec: 4 (over x_hi, core), dev: 32 (over z, y, x_lo).
Axes of the slice: x: 4 (x_hi: 2, x_lo: 2; x = x_hi * 2 + x_lo), y: 4, z: 4, core: 2. Of those that a mesh axis runs over, the one named last changes fastest.
Arguments:
- queries: bfloat16 [1024, 64, 576], P(('sec', 'dev')), may hold values from -6 to 6
- latent_cache: bfloat16 [1024, 1024, 576], P(('sec', 'dev')), may hold values from -9 to 9
- cache_length: int32 [1024], P(('sec', 'dev')), may hold values from 2 to 1024, as said below
- residual: bfloat16 [1024, 7168], P(('sec', 'dev')), may hold values from -9 to 9
- norm_gain: float32 [7168], replicated, may hold values from 0.1 to 1.9
- value_up: bfloat16 [64, 512, 128], P('dev'), may hold values from -4 to 4
- out_weight: bfloat16 [8192, 7168], P('dev'), may hold values from -0.0625 to 0.0625
- gate_weight: bfloat16 [7168, 8192], P(None, 'dev'), may hold values from -0.0625 to 0.0625
- up_weight: bfloat16 [7168, 8192], P(None, 'dev'), may hold values from -0.0625 to 0.0625
- down_weight: bfloat16 [8192, 7168], P('dev'), may hold values from -0.125 to 0.125
- expert_index: int32 [1024, 2], P(('sec', 'dev')), may hold values from 0 to 3, all different within a row; in each aligned block of 4 rows (0 to 3, 4 to 7, ...) at most 3 rows name the same one
- gate_level: int32 [1024, 2], P(('sec', 'dev')), may hold values from 1 to 4095
Outputs:
- layer_output: bfloat16 [1024, 7168], P(('sec', 'dev'))
Inputs may be any that keep to these rules, and one draw needn't show every extreme that they name: `expert_index`: each token names 2 different experts. The rows of one device form 2 aligned blocks of 4 rows, and within such a block no expert is named more than 3 times. `cache_length`: some request of the first 3 sections holds exactly 1024 live positions.
All inputs are finite; a program needn't handle non-finite values.
Results may differ from a plain program's by a relative error of at most 0.03.
Values may be sent and summed in bfloat16 or wider, within the bound.
A program may use at most 192 MiB of HBM per device.

v0:
```python
import jax
import jax.numpy as jnp
from jax import lax
from jax.sharding import PartitionSpec as P

EXPERTS = 4
TOPK = 2
MICRO = 2
CAP = 3


def from_behind(x, axis, by):
    length = lax.axis_size(axis)
    pairs = [(i, i + by) for i in range(length) if 0 <= i + by < length]
    return lax.ppermute(x, axis, pairs)


def expert_block(expert_rows, gate_weight, up_weight, down_weight):
    gate_hidden = jnp.dot(expert_rows, gate_weight, preferred_element_type=jnp.float32)
    up_hidden = jnp.dot(expert_rows, up_weight, preferred_element_type=jnp.float32)
    activated = (jax.nn.silu(gate_hidden) * up_hidden).astype(jnp.bfloat16)
    return jnp.dot(activated, down_weight, preferred_element_type=jnp.float32).astype(jnp.bfloat16)


def layer_block(
    queries,
    latent_cache,
    cache_length,
    residual,
    norm_gain,
    value_up,
    out_weight,
    gate_weight,
    up_weight,
    down_weight,
    expert_index,
    gate_level,
    groups,
):
    sections = lax.axis_size("sec")
    group_size = lax.axis_size("dev")
    section_index = lax.axis_index("sec")
    attending = section_index < sections - 1
    token_count = queries.shape[0]
    latent_width = value_up.shape[1]
    score_scale = (value_up.shape[2] + queries.shape[2] - latent_width) ** (-0.5)
    width = residual.shape[1]
    scores = (
        jnp.einsum("thc,tpc->thp", queries, latent_cache, preferred_element_type=jnp.float32)
        * score_scale
    )
    position = lax.broadcasted_iota(jnp.int32, (1, 1, latent_cache.shape[1]), 2)
    usable = position < cache_length[:, None, None]
    masked = jnp.where(usable, scores, -1e30)
    highest = jnp.max(masked, axis=2, keepdims=True)
    expos = jnp.where(usable, jnp.exp(masked - highest), 0.0)
    weights = (expos / jnp.sum(expos, axis=2, keepdims=True)).astype(jnp.bfloat16)
    latent_out = jnp.einsum(
        "thp,tpc->thc", weights, latent_cache, preferred_element_type=jnp.float32
    )[:, :, :latent_width].astype(jnp.bfloat16)
    by_heads = lax.all_to_all(latent_out, "dev", split_axis=1, concat_axis=0, tiled=True)
    head_out = jnp.einsum(
        "thc,hcv->thv", by_heads, value_up, preferred_element_type=jnp.float32
    ).astype(jnp.bfloat16)
    head_flat = head_out.reshape(head_out.shape[0], -1)
    attended = lax.psum_scatter(
        jnp.dot(head_flat, out_weight, preferred_element_type=jnp.float32).astype(jnp.bfloat16),
        "dev",
        scatter_dimension=0,
        tiled=True,
    ).astype(jnp.float32)
    stream = (residual.astype(jnp.float32) + attended).astype(jnp.bfloat16)
    stream_float = stream.astype(jnp.float32)
    mean_square = jnp.mean(stream_float * stream_float, axis=1, keepdims=True)
    normed = (stream_float * lax.rsqrt(mean_square + 1e-06) * norm_gain).astype(jnp.bfloat16)
    route_count = token_count * TOPK
    per_micro = token_count // groups
    slot_width = groups * CAP
    flat_expert = expert_index.reshape(route_count)
    route_order = jnp.arange(route_count, dtype=jnp.int32)
    micro_of = route_order // TOPK // per_micro
    earlier = (
        (route_order[:, None] > route_order[None, :])
        & (flat_expert[:, None] == flat_expert[None, :])
        & (micro_of[:, None] == micro_of[None, :])
    )
    rank_in = jnp.sum(earlier.astype(jnp.int32), axis=1)
    target = (flat_expert * slot_width + micro_of * CAP + rank_in).reshape(token_count, TOPK)
    slot_index = jnp.arange(EXPERTS * slot_width, dtype=jnp.int32)
    placing = jnp.any(slot_index[:, None, None] == target[None, :, :], axis=2).astype(jnp.bfloat16)
    levels = gate_level.astype(jnp.float32)
    mix = levels / jnp.sum(levels, axis=1, keepdims=True)
    gathering = jnp.sum(
        jnp.where(slot_index[None, None, :] == target[:, :, None], mix[:, :, None], 0.0), axis=1
    )
    packed = jnp.dot(placing, normed, preferred_element_type=jnp.float32)
    packed = jnp.where(attending, packed, 0.0).astype(jnp.bfloat16)
    slab_count = group_size // EXPERTS
    last_section = sections - 1
    pieces = []
    for source in range(last_section):
        pieces.append(from_behind(packed, "sec", last_section - source))
    stacked = jnp.stack(pieces, axis=0).reshape(last_section, EXPERTS, 1, slot_width, width)
    spread = jnp.broadcast_to(stacked, (last_section, EXPERTS, slab_count, slot_width, width))
    spread = jnp.transpose(spread, (1, 2, 0, 3, 4)).reshape(
        group_size, last_section, slot_width, width
    )
    arrived = lax.all_to_all(spread, "dev", split_axis=0, concat_axis=0, tiled=True)
    partial_out = expert_block(arrived.reshape(-1, width), gate_weight, up_weight, down_weight)
    back = lax.all_to_all(
        partial_out.reshape(group_size, last_section, slot_width, width),
        "dev",
        split_axis=0,
        concat_axis=0,
        tiled=True,
    )
    from_flat = jnp.zeros((group_size, slot_width, width), jnp.bfloat16)
    for source in range(last_section):
        moved = from_behind(back[:, source], "sec", source - last_section)
        from_flat = jnp.where(section_index == source, moved, from_flat)
    from_experts = from_flat.reshape(EXPERTS, slab_count, slot_width, width)
    slab_total = jnp.sum(from_experts.astype(jnp.float32), axis=1).reshape(
        EXPERTS * slot_width, width
    )
    moe = jnp.dot(gathering, slab_total, precision=lax.Precision.HIGHEST)
    result = (stream_float + moe).astype(jnp.bfloat16)
    return jnp.where(attending, result, jnp.zeros_like(result))


def body(
    queries,
    latent_cache,
    cache_length,
    residual,
    norm_gain,
    value_up,
    out_weight,
    gate_weight,
    up_weight,
    down_weight,
    expert_index,
    gate_level,
):
    return layer_block(
        queries,
        latent_cache,
        cache_length,
        residual,
        norm_gain,
        value_up,
        out_weight,
        gate_weight,
        up_weight,
        down_weight,
        expert_index,
        gate_level,
        MICRO,
    )


def solution(mesh):
    placed = (
        P(("sec", "dev"), None, None),
        P(("sec", "dev"), None, None),
        P(("sec", "dev")),
        P(("sec", "dev"), None),
        P(),
        P("dev", None, None),
        P("dev", None),
        P(None, "dev"),
        P(None, "dev"),
        P("dev", None),
        P(("sec", "dev"), None),
        P(("sec", "dev"), None),
    )
    return jax.shard_map(
        body, mesh=mesh, in_specs=placed, out_specs=P(("sec", "dev"), None), check_vma=False
    )
```

profile of v0, /device:TPU:0, one launch (start us, length us, event | category | flops | bytes accessed | tf_op | source)
XLA Modules:
  0.0 691.1 jit_solution(9540365093698168124)
XLA Ops:
  6.5 0.8 iota_compare_fusion
  7.6 6.0 fusion.32
  13.6 6.6 fusion.6
  20.6 21.5 %all_to_all.28 = bf16[8,64,512]{2,0,1:T(8,128)(2,1)S(1)} all-to-all(bf16[8,64,512]{2,0,1:T(8,128)(2,1)S(1)} %copy.49), channel_id=1, replica_groups=mesh['sec'=4,'dev'=32] {'dev'}, dimensions={1} | all-to-all | bytes 1048576 | tf_op jit(solution)/shard_map/all_to_all | solution.py:61
  42.5 2.9 convolution_convert_fusion.1
  45.5 0.6 copy-done.5
  46.8 168.3 %reduce-scatter.2.cloned.1.call-done = bf16[8,7168]{1,0:T(8,128)(2,1)} async-done(((bf16[256,7168]{1,0:T(8,128)(2,1)}), bf16[8,7168]{1,0:T(8,128)(2,1)}) %reduce-scatter.2.cloned.1.call-update) | async-done | bytes 114704 | tf_op jit(solution)/shard_map/reduce_scatter | solution.py:66
  215.1 1.1 fusion.13
  216.2 1.2 fusion.1
  217.4 1.3 collective-permute-start
  218.7 3.6 collective-permute-start.1
  222.3 1.3 collective-permute-start.2
  223.8 6.3 collective-permute-done.1
  230.8 5.4 broadcast_in_dim.67
  236.2 132.8 %all_to_all.29 = bf16[32,3,6,7168]{3,2,1,0:T(8,128)(2,1)} all-to-all(bf16[32,3,6,7168]{3,2,1,0:T(8,128)(2,1)} %bitcast.46), channel_id=1, replica_groups=mesh['sec'=4,'dev'=32] {'dev'}, dimensions={0} | all-to-all | bytes 16515072 | tf_op jit(solution)/shard_map/all_to_all | solution.py:108
  369.0 12.5 %reshape.218 = bf16[576,7168]{1,0:T(8,128)(2,1)} reshape(bf16[32,3,6,7168]{3,2,1,0:T(8,128)(2,1)} %all_to_all.29) | data formatting | bytes 16515072 | tf_op jit(solution)/shard_map/reshape | solution.py:109
  381.5 6.7 fusion.35
  388.2 17.4 %convolution_convert_fusion = bf16[576,7168]{1,0:T(8,128)(2,1)} fusion(bf16[256,7168]{1,0:T(8,128)(2,1)} %param.21, bf16[576,7168]{1,0:T(8,128)(2,1)} %reshape.218, bf16[7168,256]{1,0:T(8,128)(2,1)} %param.20, f32[576,256]{1,0:T(8,128)S(1)} %fusion.35), kind=kOutput, calls=%fused_computation.1 | convolution fusion | flops 4232871936 | bytes 24444928 | tf_op jit(solution)/shard_map/dot_general | solution.py:22
  405.6 11.6 %reshape.219 = bf16[32,3,6,7168]{3,2,1,0:T(8,128)(2,1)} reshape(bf16[576,7168]{1,0:T(8,128)(2,1)} %convolution_convert_fusion) | data formatting | bytes 16515072 | tf_op jit(solution)/shard_map/reshape | solution.py:111
  417.2 132.9 %all_to_all.30 = bf16[32,3,6,7168]{3,2,1,0:T(8,128)(2,1)S(1)} all-to-all(bf16[32,3,6,7168]{3,2,1,0:T(8,128)(2,1)} %reshape.219), channel_id=1, replica_groups=mesh['sec'=4,'dev'=32] {'dev'}, dimensions={0} | all-to-all | bytes 16515072 | tf_op jit(solution)/shard_map/all_to_all | solution.py:110
  550.2 0.9 slice_bitcast_fusion
  551.1 3.1 copy.57
  554.2 1.5 collective-permute-start.3
  555.7 3.1 copy.58
  558.7 1.4 collective-permute-start.4
  560.1 3.2 copy.59
  563.3 1.3 collective-permute-start.5
  564.7 105.6 %collective-permute-done.4 = bf16[32,6,7168]{2,0,1:T(8,128)(2,1)} collective-permute-done((bf16[32,6,7168]{2,0,1:T(8,128)(2,1)}, bf16[32,6,7168]{2,0,1:T(8,128)(2,1)}, u32[]{:S(2)}, u32[]{:S(2)}) %collective-permute-start.4) | collective-permute-done | bytes 2752544 | tf_op jit(solution)/shard_map/ppermute | solution.py:15
  670.3 7.0 %collective-permute-done.5 = bf16[32,6,7168]{2,0,1:T(8,128)(2,1)} collective-permute-done((bf16[32,6,7168]{2,0,1:T(8,128)(2,1)}, bf16[32,6,7168]{2,0,1:T(8,128)(2,1)}, u32[]{:S(2)}, u32[]{:S(2)}) %collective-permute-start.5) | collective-permute-done | bytes 2752544 | tf_op jit(solution)/shard_map/ppermute | solution.py:15
  677.3 4.4 convert_reduce_fusion
  681.7 0.4 copy.60
  682.3 2.0 fusion.3
  (41 shorter events, 2.7 us)
Async XLA Ops:
  6.5 1.1 copy-start
  6.5 208.6 %reduce-scatter.2.cloned.1.call-start = ((), (), s32[]{:S(2)}) async-start(), calls=%async_computation.4 | async-start | bytes 3784704 | tf_op jit(solution)/shard_map/reduce_scatter | solution.py:66
  13.6 28.6 %copy-start.7 = (bf16[2,512,128]{2,1,0:T(8,128)(2,1)S(1)}, bf16[2,512,128]{2,1,0:T(8,128)(2,1)}, u32[]{:S(2)}) copy-start(bf16[2,512,128]{2,1,0:T(8,128)(2,1)} %param.17) | copy-start | bytes 786436
  20.3 22.2 %copy-start.2 = (bf16[256,7168]{1,0:T(8,128)(2,1)S(1)}, bf16[256,7168]{1,0:T(8,128)(2,1)}, u32[]{:S(2)}) copy-start(bf16[256,7168]{1,0:T(8,128)(2,1)} %param.18) | copy-start | bytes 11010052
  45.5 0.7 copy-start.5
  45.5 169.6 %copy-start.3 = (bf16[8,7168]{1,0:T(8,128)(2,1)S(1)}, bf16[8,7168]{1,0:T(8,128)(2,1)}, u32[]{:S(2)}) copy-start(bf16[8,7168]{1,0:T(8,128)(2,1)} %param.15) | copy-start | bytes 344068
  45.5 170.7 %copy-start.4 = (f32[7168]{0:T(1024)S(1)}, f32[7168]{0:T(1024)}, u32[]{:S(2)}) copy-start(f32[7168]{0:T(1024)} %param.16) | copy-start | bytes 86020
  217.4 6.3 collective-permute-start
  218.7 11.4 %collective-permute-start.1 = (bf16[24,7168]{1,0:T(8,128)(2,1)S(1)}, bf16[24,7168]{1,0:T(8,128)(2,1)S(1)}, u32[]{:S(2)}, u32[]{:S(2)}) collective-permute-start(bf16[24,7168]{1,0:T(8,128)(2,1)S(1)} %fusion.1), channel_id=1, source_target_pairs={{0,64},{32,96},{1,65},{33,97},{2,66},{34,98},{3,67},{35,99},{4,68}... | collective-permute-start | bytes 1032200 | tf_op jit(solution)/shard_map/ppermute | solution.py:15
  222.3 7.9 %collective-permute-start.2 = (bf16[24,7168]{1,0:T(8,128)(2,1)S(1)}, bf16[24,7168]{1,0:T(8,128)(2,1)S(1)}, u32[]{:S(2)}, u32[]{:S(2)}) collective-permute-start(bf16[24,7168]{1,0:T(8,128)(2,1)S(1)} %fusion.1), channel_id=1, source_target_pairs={{0,32},{32,64},{64,96},{1,33},{33,65},{65,97},{2,34},{34,66},{66,9... | collective-permute-start | bytes 1032200 | tf_op jit(solution)/shard_map/ppermute | solution.py:15
  554.2 10.6 %collective-permute-start.3 = (bf16[32,6,7168]{2,0,1:T(8,128)(2,1)}, bf16[32,6,7168]{2,0,1:T(8,128)(2,1)S(1)}, u32[]{:S(2)}, u32[]{:S(2)}) collective-permute-start(bf16[32,6,7168]{2,0,1:T(8,128)(2,1)} %copy.57), channel_id=1, source_target_pairs={{32,0},{64,32},{96,64},{33,1},{65,33},{97,65},{34,2},{66,34},{98,6... | collective-permute-start | bytes 8257544 | tf_op jit(solution)/shard_map/ppermute | solution.py:15
  558.7 5.9 copy-start.6
  558.7 111.6 %collective-permute-start.4 = (bf16[32,6,7168]{2,0,1:T(8,128)(2,1)}, bf16[32,6,7168]{2,0,1:T(8,128)(2,1)}, u32[]{:S(2)}, u32[]{:S(2)}) collective-permute-start(bf16[32,6,7168]{2,0,1:T(8,128)(2,1)} %copy.58), channel_id=1, source_target_pairs={{64,0},{96,32},{65,1},{97,33},{66,2},{98,34},{67,3},{99,35},{68,4}... | collective-permute-start | bytes 8257544 | tf_op jit(solution)/shard_map/ppermute | solution.py:15
  563.3 114.0 %collective-permute-start.5 = (bf16[32,6,7168]{2,0,1:T(8,128)(2,1)}, bf16[32,6,7168]{2,0,1:T(8,128)(2,1)}, u32[]{:S(2)}, u32[]{:S(2)}) collective-permute-start(bf16[32,6,7168]{2,0,1:T(8,128)(2,1)} %copy.59), channel_id=1, source_target_pairs={{96,0},{97,1},{98,2},{99,3},{100,4},{101,5},{102,6},{103,7},{104,8... | collective-permute-start | bytes 8257544 | tf_op jit(solution)/shard_map/ppermute | solution.py:15
  677.3 7.0 %copy-start.1 = (bf16[8,64,576]{2,1,0:T(8,128)(2,1)S(1)}, bf16[8,64,576]{2,1,0:T(8,128)(2,1)}, u32[]{:S(2)}) copy-start(bf16[8,64,576]{2,1,0:T(8,128)(2,1)} %param.12) | copy-start | bytes 1769476
Sparse Core Ops, SparseCore 0:
  45.6 169.4 reduce-scatter.1
where the time goes:
time: 692 us; the launch traced here: 691 us
  blocking collectives  287 us (41%)
  waiting for transfers between devices  287 us (41%)
  matrix products  43.2 us (6%)
  local copies, waits for them, and re-layouts  42.3 us (6%)
  between operations  13.6 us (2%)
  starting transfers between devices  10.4 us (2%)
  other arithmetic  7.04 us (1%)
    reduce_scatter x1, waiting for transfers between devices, layer_block(): lax.psum_scatter(jnp.dot(head_flat, out_weight, preferred_element_type=jn...  168 us
    all_to_all x1, blocking collectives, layer_block(): lax.all_to_all(partial_out.reshape(group_size, last_section, slot_width,...  133 us
    all_to_all x1, blocking collectives, layer_block(): lax.all_to_all(spread, 'dev', split_axis=0, concat_axis=0, tiled=True)  133 us
    ppermute x6, waiting for transfers between devices, from_behind(): return lax.ppermute(x, axis, pairs)  119 us
    all_to_all x1, blocking collectives, layer_block(): lax.all_to_all(latent_out, 'dev', split_axis=1, concat_axis=0, tiled=True)  21.5 us
    dot_general x1, matrix products, expert_block(): jnp.dot(activated, down_weight, preferred_element_type=jnp.float32)  17.4 us
  transfers between devices with their start and end apart: 7, of which 4 were waited for; matrix products, arithmetic and copies ran while one was open for 1% of the time, Pallas kernels for 0%

commit v1 on v0

v1 whole, which is shorter than its diff:
```python
import functools

import jax
import jax.numpy as jnp
from jax import lax
from jax.experimental import pallas as pl
from jax.experimental.pallas import tpu as pltpu
from jax.sharding import PartitionSpec as P

EXPERTS = 4
TOPK = 2
ROWS = 8
GROUP = 32
DIMS = 5
TILE = 256
MASKS = (1, 2, 6, 8, 24)
STEP_AT = (0, 16, 24, 28, 30)
MESH = pl.DeviceIdType.MESH


def mask_of(code):
    mask = 0
    for dim in range(DIMS):
        if (code >> dim) & 1:
            mask ^= MASKS[dim]
    return mask


def order_of(chunk):
    return [(chunk + step) % DIMS for step in range(DIMS)]


def place_of(chunk, code):
    place = 0
    for step, dim in enumerate(order_of(chunk)):
        place += ((code >> dim) & 1) << (DIMS - 1 - step)
    return place


def flipped(bits, mask):
    total = 0
    for i, bit in enumerate(bits):
        total = total + (1 << i) * ((1 - bit) if (mask >> i) & 1 else bit)
    return total


def layer_kernel(
    widths,
    head_ref,
    residual_ref,
    gain_ref,
    share_ref,
    out_weight_hbm,
    gate_hbm,
    up_hbm,
    down_hbm,
    out_ref,
    out_weight,
    gate,
    up,
    down,
    wide,
    left,
    stream,
    gate_sum,
    up_sum,
    act,
    load_sem,
    send_sem,
    recv_sem,
    *buffers,
):
    chunks = len(widths)
    partial = buffers[:chunks]
    landing = buffers[chunks : 2 * chunks]
    landing_two = buffers[2 * chunks : 3 * chunks]
    rows_of = buffers[3 * chunks :]
    starts = [sum(widths[:k]) for k in range(chunks)]
    section = lax.axis_index("sec")
    me = lax.axis_index("dev")
    bits = [(me // (1 << i)) % 2 for i in range(DIMS)]
    partners = [flipped(bits, mask) for mask in MASKS]

    loads = []
    for i, (source, target) in enumerate(
        ((out_weight_hbm, out_weight), (gate_hbm, gate), (up_hbm, up), (down_hbm, down))
    ):
        load = pltpu.make_async_copy(source, target, load_sem.at[i])
        load.start()
        loads.append(load)

    barrier = pltpu.get_barrier_semaphore()
    for partner in partners:
        pl.semaphore_signal(barrier, inc=1, device_id=(section, partner), device_id_type=MESH)
    pl.semaphore_wait(barrier, DIMS)

    def send(source, target, phase, chunk, step, dim):
        copy = pltpu.make_async_remote_copy(
            src_ref=source,
            dst_ref=target,
            send_sem=send_sem.at[phase, chunk, step],
            recv_sem=recv_sem.at[phase, chunk, step],
            device_id=(section, partners[dim]),
            device_id_type=MESH,
        )
        copy.start()
        return copy

    def reduce_send(phase, chunk, step, arrivals):
        half = 16 >> step
        return send(
            partial[chunk].at[pl.ds(half, half)],
            arrivals[chunk].at[pl.ds(STEP_AT[step], half)],
            phase,
            chunk,
            step,
            order_of(chunk)[step],
        )

    def add_rows(chunk, arrivals, at, first, count):
        @pl.loop(0, count)
        def _(i):
            row = first + i
            partial[chunk][row] = partial[chunk][row] + arrivals[chunk][at + row]

    def reduce_scatter(phase, copies, arrivals):
        started = list(copies)
        current = list(copies)
        for step in range(DIMS):
            half = 16 >> step
            for chunk in range(chunks):
                current[chunk].wait_recv()
                if step < DIMS - 1:
                    add_rows(chunk, arrivals, STEP_AT[step], half // 2, half // 2)
                    current[chunk] = reduce_send(phase, chunk, step + 1, arrivals)
                    started.append(current[chunk])
                    add_rows(chunk, arrivals, STEP_AT[step], 0, half // 2)
                else:
                    add_rows(chunk, arrivals, STEP_AT[step], 0, 1)
        return started

    def project(chunk, operand, weight, scale):
        @pl.loop(0, widths[chunk] // TILE)
        def _(i):
            inner = pl.ds(pl.multiple_of(i * TILE, TILE), TILE)
            outer = pl.ds(pl.multiple_of(starts[chunk] + i * TILE, TILE), TILE)
            product = jnp.dot(operand[...], weight[:, outer], preferred_element_type=jnp.float32)
            if scale is not None:
                product = product * scale
            for code in range(GROUP):
                block = product[code * ROWS : (code + 1) * ROWS]
                partial[chunk][place_of(chunk, code), :, inner] = block.astype(jnp.bfloat16)

    for code in range(GROUP):
        block = head_ref[flipped(bits, mask_of(code))].astype(jnp.float32)
        wide[code * ROWS : (code + 1) * ROWS] = block
    left[...] = wide[...].astype(jnp.bfloat16)
    loads[0].wait()
    copies = []
    for chunk in range(chunks):
        project(chunk, left, out_weight, None)
        copies.append(reduce_send(0, chunk, 0, landing))
    started = reduce_scatter(0, copies, landing)

    square = jnp.zeros((ROWS, 1), jnp.float32)
    for chunk in range(chunks):
        columns = pl.ds(starts[chunk], widths[chunk])
        attended = partial[chunk][0].astype(jnp.float32)
        total = (residual_ref[:, columns].astype(jnp.float32) + attended).astype(jnp.bfloat16)
        stream[:, columns] = total
        total = total.astype(jnp.float32)
        square = square + jnp.sum(total * total, axis=1, keepdims=True)
    level = lax.rsqrt(square / stream.shape[1] + 1e-06)
    gathers = [[] for _ in range(chunks)]

    def gather_send(chunk, step):
        count = 1 << step
        copy = send(
            rows_of[chunk].at[pl.ds(0, count)],
            rows_of[chunk].at[pl.ds(count, count)],
            1,
            chunk,
            step,
            order_of(chunk)[DIMS - 1 - step],
        )
        gathers[chunk].append(copy)

    for chunk in range(chunks):
        columns = pl.ds(starts[chunk], widths[chunk])
        normed = stream[:, columns].astype(jnp.float32) * level * gain_ref[:, columns]
        rows_of[chunk][0, :, : widths[chunk]] = normed.astype(jnp.bfloat16)
        if chunk == chunks - 1:
            rows_of[chunk][0, :, widths[chunk] :] = share_ref[...]
        gather_send(chunk, 0)
    for step in range(1, DIMS):
        for chunk in range(chunks):
            gathers[chunk][step - 1].wait_recv()
            gather_send(chunk, step)
    gate_sum[...] = jnp.zeros_like(gate_sum)
    up_sum[...] = jnp.zeros_like(up_sum)
    loads[1].wait()
    loads[2].wait()

    def stacked(chunk, columns):
        blocks = [
            rows_of[chunk][place_of(chunk, code), :, columns].astype(jnp.float32)
            for code in range(GROUP)
        ]
        return jnp.concatenate(blocks, axis=0)

    for chunk in range(chunks):
        gathers[chunk][DIMS - 1].wait_recv()

        @pl.loop(0, widths[chunk] // TILE)
        def _(i):
            inner = pl.ds(pl.multiple_of(i * TILE, TILE), TILE)
            outer = pl.ds(pl.multiple_of(starts[chunk] + i * TILE, TILE), TILE)
            rows = stacked(chunk, inner).astype(jnp.bfloat16)
            gate_sum[...] += jnp.dot(rows, gate[outer, :], preferred_element_type=jnp.float32)
            up_sum[...] += jnp.dot(rows, up[outer, :], preferred_element_type=jnp.float32)

    shares = stacked(chunks - 1, pl.ds(widths[chunks - 1], 128))
    lane = lax.broadcasted_iota(jnp.int32, shares.shape, 1)
    expert = me // (GROUP // EXPERTS)
    share = jnp.sum(
        jnp.where((lane == expert) | (lane == expert + EXPERTS), shares, 0.0), axis=1, keepdims=True
    )
    hidden = gate_sum[...]
    act[...] = (hidden / (1.0 + jnp.exp(-hidden)) * up_sum[...]).astype(jnp.bfloat16)
    loads[3].wait()
    for copy in started:
        copy.wait_send()
    copies = []
    for chunk in range(chunks):
        project(chunk, act, down, share)
        copies.append(reduce_send(2, chunk, 0, landing_two))
    started = reduce_scatter(2, copies, landing_two)
    for chunk in range(chunks):
        columns = pl.ds(starts[chunk], widths[chunk])
        result = stream[:, columns].astype(jnp.float32) + partial[chunk][0].astype(jnp.float32)
        result = jnp.where(section < lax.axis_size("sec") - 1, result, 0.0)
        out_ref[:, columns] = result.astype(jnp.bfloat16)
    for chunk in range(chunks):
        for copy in gathers[chunk]:
            copy.wait_send()
    for copy in started:
        copy.wait_send()


def layer_tail(heads, residual, gain, shares, out_weight, gate_weight, up_weight, down_weight):
    width = residual.shape[1]
    tiles = width // TILE
    widths = [TILE * (tiles // DIMS + (1 if k < tiles % DIMS else 0)) for k in range(DIMS)]
    hidden = gate_weight.shape[1]
    bf16, f32 = jnp.bfloat16, jnp.float32
    vmem = pl.BlockSpec(memory_space=pltpu.VMEM)
    hbm = pl.BlockSpec(memory_space=pl.ANY)
    scratch = [
        pltpu.VMEM(out_weight.shape, bf16),
        pltpu.VMEM(gate_weight.shape, bf16),
        pltpu.VMEM(up_weight.shape, bf16),
        pltpu.VMEM(down_weight.shape, bf16),
        pltpu.VMEM((GROUP * ROWS, heads.shape[2]), f32),
        pltpu.VMEM((GROUP * ROWS, heads.shape[2]), bf16),
        pltpu.VMEM((ROWS, width), bf16),
        pltpu.VMEM((GROUP * ROWS, hidden), f32),
        pltpu.VMEM((GROUP * ROWS, hidden), f32),
        pltpu.VMEM((GROUP * ROWS, hidden), bf16),
        pltpu.SemaphoreType.DMA((4,)),
        pltpu.SemaphoreType.DMA((3, DIMS, DIMS)),
        pltpu.SemaphoreType.DMA((3, DIMS, DIMS)),
    ]
    scratch += [pltpu.VMEM((GROUP, ROWS, w), bf16) for w in widths]
    scratch += [pltpu.VMEM((GROUP - 1, ROWS, w), bf16) for w in widths] * 2
    extra = [0] * (DIMS - 1) + [128]
    scratch += [pltpu.VMEM((GROUP, ROWS, w + e), bf16) for w, e in zip(widths, extra)]
    return pl.pallas_call(
        functools.partial(layer_kernel, widths),
        out_shape=jax.ShapeDtypeStruct(residual.shape, bf16),
        in_specs=[vmem] * 4 + [hbm] * 4,
        out_specs=vmem,
        scratch_shapes=scratch,
        compiler_params=pltpu.CompilerParams(
            collective_id=0, has_side_effects=True, vmem_limit_bytes=56 * 1024 * 1024
        ),
    )(heads, residual, gain, shares, out_weight, gate_weight, up_weight, down_weight)


def body(
    queries,
    latent_cache,
    cache_length,
    residual,
    norm_gain,
    value_up,
    out_weight,
    gate_weight,
    up_weight,
    down_weight,
    expert_index,
    gate_level,
):
    latent_width = value_up.shape[1]
    score_scale = (value_up.shape[2] + queries.shape[2] - latent_width) ** (-0.5)
    scores = (
        jnp.einsum("thc,tpc->thp", queries, latent_cache, preferred_element_type=jnp.float32)
        * score_scale
    )
    position = lax.broadcasted_iota(jnp.int32, (1, 1, latent_cache.shape[1]), 2)
    usable = position < cache_length[:, None, None]
    masked = jnp.where(usable, scores, -1e30)
    highest = jnp.max(masked, axis=2, keepdims=True)
    expos = jnp.where(usable, jnp.exp(masked - highest), 0.0)
    weights = (expos / jnp.sum(expos, axis=2, keepdims=True)).astype(jnp.bfloat16)
    latent_out = jnp.einsum(
        "thp,tpc->thc", weights, latent_cache, preferred_element_type=jnp.float32
    )[:, :, :latent_width].astype(jnp.bfloat16)
    by_heads = lax.all_to_all(latent_out, "dev", split_axis=1, concat_axis=0, tiled=True)
    head_out = jnp.einsum(
        "thc,hcv->thv", by_heads, value_up, preferred_element_type=jnp.float32
    ).astype(jnp.bfloat16)
    heads = head_out.reshape(GROUP, ROWS, -1)

    levels = gate_level.astype(jnp.float32)
    mix = levels / jnp.sum(levels, axis=1, keepdims=True)
    named = expert_index[:, :, None] == jnp.arange(EXPERTS, dtype=jnp.int32)[None, None, :]
    share = jnp.sum(jnp.where(named, mix[:, :, None], 0.0), axis=1)
    coarse = share.astype(jnp.bfloat16)
    fine = (share - coarse.astype(jnp.float32)).astype(jnp.bfloat16)
    shares = jnp.pad(jnp.concatenate([coarse, fine], axis=1), ((0, 0), (0, 128 - 2 * EXPERTS)))
    return layer_tail(
        heads,
        residual,
        norm_gain.reshape(1, -1),
        shares,
        out_weight,
        gate_weight,
        up_weight,
        down_weight,
    )


def solution(mesh):
    placed = (
        P(("sec", "dev"), None, None),
        P(("sec", "dev"), None, None),
        P(("sec", "dev")),
        P(("sec", "dev"), None),
        P(),
        P("dev", None, None),
        P("dev", None),
        P(None, "dev"),
        P(None, "dev"),
        P("dev", None),
        P(("sec", "dev"), None),
        P(("sec", "dev"), None),
    )
    return jax.shard_map(
        body, mesh=mesh, in_specs=placed, out_specs=P(("sec", "dev"), None), check_vma=False
    )
```

time: 692 us -> 133 us (0.19)
  blocking collectives: 287 us -> 0 us
  waiting for transfers between devices: 287 us -> 11.3 us
  Pallas kernels: 0 us -> 93.4 us
  local copies, waits for them, and re-layouts: 42.3 us -> 4.04 us
  matrix products: 43.2 us -> 12.9 us
  between operations: 13.6 us -> 0.1 us
    all_to_all x3 -> x0, blocking collectives: 287 us -> none  [the longest x1 133 us: layer_block(): lax.all_to_all(partial_out.reshape(group_size, last_section, slot_width,...]
    reduce_scatter x1 -> x0, waiting for transfers between devices: 168 us -> none  [layer_block(): lax.psum_scatter(jnp.dot(head_flat, out_weight, preferred_element_type=jn...]
    ppermute x6 -> x0, waiting for transfers between devices: 119 us -> none  [from_behind(): return lax.ppermute(x, axis, pairs)]
    pallas_call x0 -> x1, Pallas kernels: none -> 93.4 us  [layer_tail(): pl.pallas_call(functools.partial(layer_kernel, widths), out_shape=jax.Sha...]
    dot_general x7 -> x2, matrix products: 37.2 us -> 6.89 us  [the longest x1 6.6 us: body(): jnp.einsum('thp,tpc->thc', weights, latent_cache, preferred_element_type=...]
    reshape x3 -> x1, local copies, waits for them, and re-layouts: 24.2 us -> 0.73 us  [body(): heads = head_out.reshape(GROUP, ROWS, -1)]
    all_to_all x0 -> x1, waiting for transfers between devices: none -> 11.3 us  [body(): lax.all_to_all(latent_out, 'dev', split_axis=1, concat_axis=0, tiled=True)]
    ppermute x6 -> x0, starting transfers between devices: 10.4 us -> none  [from_behind(): return lax.ppermute(x, axis, pairs)]
  transfers between devices with their start and end apart: 7 -> 1, of which waited for: 4 -> 1; matrix products, arithmetic and copies ran while one was open for 1% -> 1% of each run, Pallas kernels for 0% -> 0%
where the time goes in v1:
time: 133 us
  Pallas kernels  93.4 us (70%)
  matrix products  12.9 us (10%)
  waiting for transfers between devices  11.3 us (8%)
  starting transfers between devices  9.34 us (7%)
  local copies, waits for them, and re-layouts  4.04 us (3%)
  other arithmetic  1.5 us (1%)
    pallas_call x1, Pallas kernels, layer_tail(): pl.pallas_call(functools.partial(layer_kernel, widths), out_shape=jax.Sha...  93.4 us
    all_to_all x1, waiting for transfers between devices, body(): lax.all_to_all(latent_out, 'dev', split_axis=1, concat_axis=0, tiled=True)  11.3 us
    all_to_all x1, starting transfers between devices, body(): lax.all_to_all(latent_out, 'dev', split_axis=1, concat_axis=0, tiled=True)  9.34 us
    dot_general x1, matrix products, body(): jnp.einsum('thp,tpc->thc', weights, latent_cache, preferred_element_type=...  6.6 us
    sub x1, matrix products, body(): expos = jnp.where(usable, jnp.exp(masked - highest), 0.0)  6 us
  transfers between devices with their start and end apart: 1, of which 1 were waited for; matrix products, arithmetic and copies ran while one was open for 1% of the time, Pallas kernels for 0%

profile of v1, /device:TPU:0, one launch (start us, length us, event | category | flops | bytes accessed | tf_op | source)
XLA Modules:
  0.0 132.6 jit_solution(425857194527917819)
XLA Ops:
  0.0 0.0 copy-start
  0.0 0.8 iota_compare_fusion
  0.8 0.3 copy-done
  1.1 6.0 %fusion.15 = (f32[8,64]{1,0:T(8,128)S(1)}, f32[8,64,1024]{2,1,0:T(8,128)S(1)}) fusion(pred[8,1024]{1,0:T(8,128)(4,1)S(1)} %iota_compare_fusion, bf16[8,64,576]{2,1,0:T(8,128)(2,1)S(1)} %copy-done, bf16[8,1024,576]{1,2,0:T(8,128)(2,1)} %param.13), kind=kOutput, calls=%fused_computation.27 | convolution fusion | flops 606602240 | bytes 12134400 | tf_op jit(solution)/shard_map/sub | solution.py:313
  7.1 6.6 %fusion.3 = bf16[8,64,576]{2,1,0:T(8,128)(2,1)S(1)} fusion(bf16[8,1024,576]{1,2,0:T(8,128)(2,1)} %param.13, f32[8,64,1024]{2,1,0:T(8,128)S(1)} %get-tuple-element.6, f32[8,64]{1,0:T(8,128)S(1)} %get-tuple-element.5), kind=kOutput, calls=%fused_computation.7 | convolution fusion | flops 605028352 | bytes 12126208 | tf_op jit(solution)/shard_map/thp,tpc->thc/dot_general | solution.py:315
  13.7 0.0 copy-start.1
  13.7 0.0 copy-start.2
  13.7 0.0 copy-start.3
  13.8 1.1 copy.27
  14.9 9.3 %all-to-all-start = ((bf16[8,64,512]{2,0,1:T(8,128)(2,1)}), bf16[8,64,512]{2,0,1:T(8,128)(2,1)S(1)}, u32[]{:S(2)}, u32[]{:S(2)}) async-start(bf16[8,64,512]{2,0,1:T(8,128)(2,1)} %copy.27), calls=%async_computation | async-start | bytes 1048576 | tf_op jit(solution)/shard_map/all_to_all | solution.py:318
  24.2 0.0 copy-done.1
  24.3 0.0 copy-done.2
  24.3 0.1 copy.31
  24.4 0.1 copy.32
  24.5 0.7 fusion.12.share_ref
  25.1 11.3 %all-to-all-done = bf16[8,64,512]{2,0,1:T(8,128)(2,1)S(1)} async-done(((bf16[8,64,512]{2,0,1:T(8,128)(2,1)}), bf16[8,64,512]{2,0,1:T(8,128)(2,1)S(1)}, u32[]{:S(2)}, u32[]{:S(2)}) %all-to-all-start) | async-done | bytes 524320 | tf_op jit(solution)/shard_map/all_to_all | solution.py:318
  36.5 0.0 copy-done.3
  36.5 0.3 fusion.2
  36.8 0.1 copy.29
  36.9 0.7 reshape.32.head_ref
  37.7 93.4 %shard_map.118 = bf16[8,7168]{1,0:T(8,128)(2,1)} custom-call(bf16[32,8,256]{2,1,0:T(8,128)(2,1)} %reshape.32.head_ref, bf16[8,7168]{1,0:T(8,128)(2,1)} %residual_ref.1, f32[1,7168]{1,0:T(1,128)} %bitcast.14, bf16[8,128]{1,0:T(8,128)(2,1)} %fusion.12.share_ref, bf16[256,7168]{1,0:T(8,128)(2,1)} %out_weight_hbm.1, bf16[7168,256]{1,0:T(8,128)(2,1)} %gate_hbm.1, ...), custom_call_target="tpu_custom_call" | custom-call | tf_op jit(solution)/shard_map/pallas_call | solution.py:277
  131.1 1.6 %copy.38 = bf16[8,7168]{1,0:T(8,128)(2,1)} copy(bf16[8,7168]{1,0:T(8,128)(2,1)} %shard_map.118) | data formatting | bytes 229376
  (6 shorter events, 0.1 us)
Async XLA Ops:
  0.0 1.1 copy-start
  13.7 10.5 %copy-start.1 = (s32[8,2]{0,1:T(2,128)S(1)}, s32[8,2]{0,1:T(2,128)}, u32[]{:S(2)}) copy-start(s32[8,2]{0,1:T(2,128)} %param.23) | copy-start | bytes 196
  13.7 10.5 %copy-start.2 = (s32[8,2]{0,1:T(2,128)S(1)}, s32[8,2]{0,1:T(2,128)}, u32[]{:S(2)}) copy-start(s32[8,2]{0,1:T(2,128)} %param.22) | copy-start | bytes 196
  13.7 22.8 %copy-start.3 = (bf16[2,512,128]{2,1,0:T(8,128)(2,1)S(1)}, bf16[2,512,128]{2,1,0:T(8,128)(2,1)}, u32[]{:S(2)}) copy-start(bf16[2,512,128]{2,1,0:T(8,128)(2,1)} %param.17) | copy-start | bytes 786436
  14.9 21.6 %all-to-all-start = ((bf16[8,64,512]{2,0,1:T(8,128)(2,1)}), bf16[8,64,512]{2,0,1:T(8,128)(2,1)S(1)}, u32[]{:S(2)}, u32[]{:S(2)}) async-start(bf16[8,64,512]{2,0,1:T(8,128)(2,1)} %copy.27), calls=%async_computation | async-start | bytes 1048576 | tf_op jit(solution)/shard_map/all_to_all | solution.py:318

commit v2 on v1

v2 whole, which is shorter than its diff:
```python
import functools

import jax
import jax.numpy as jnp
from jax import lax
from jax.experimental import pallas as pl
from jax.experimental.pallas import tpu as pltpu
from jax.sharding import PartitionSpec as P

EXPERTS = 4
TOPK = 2
ROWS = 8
GROUP = 32
DIMS = 5
TILE = 256
LANES = 128
CHUNKS = 8
SPREAD = 4
SLOTS = 2 * SPREAD + 3
MASKS = (1, 2, 6, 8, 24)
MESH = pl.DeviceIdType.MESH


def mask_of(code):
    mask = 0
    for dim in range(DIMS):
        if (code >> dim) & 1:
            mask ^= MASKS[dim]
    return mask


def flipped(bits, mask):
    total = 0
    for i, bit in enumerate(bits):
        total = total + (1 << i) * ((1 - bit) if (mask >> i) & 1 else bit)
    return total


class Plan:
    def __init__(self, core):
        self.core = core
        self.blocks = GROUP if core == 0 else GROUP // 2
        self.halvings = 3 if core == 0 else 2
        self.rows = self.blocks * ROWS

    def order(self, chunk):
        turn = chunk // 2 if self.core == 0 else chunk
        ring = [1 + (turn + i) % 4 for i in range(4)]
        if self.core == 1:
            return ring
        return [0] + ring if chunk % 2 == 0 else ring + [0]

    def codes(self):
        return [(code if self.core == 0 else 2 * code) for code in range(self.blocks)]

    def place(self, chunk, code):
        order = self.order(chunk)
        place = 0
        for step, dim in enumerate(order):
            place += ((code >> dim) & 1) << (len(order) - 1 - step)
        return place

    def code(self, chunk, place):
        order = self.order(chunk)
        code = 0
        for step, dim in enumerate(order):
            code += ((place >> (len(order) - 1 - step)) & 1) << dim
        return code


def work(plan, widths, refs, buffers, loads):
    (
        latent_ref,
        residual_ref,
        gain_ref,
        share_ref,
        value_ref,
        out_ref,
        out_weight,
        gate,
        up,
        down,
        latents,
        left,
        stream,
        gate_sum,
        up_sum,
        act,
        pass_send,
        pass_recv,
        send_sem,
        recv_sem,
    ) = refs
    partial = buffers[:CHUNKS]
    landings = (buffers[CHUNKS : 2 * CHUNKS], None, buffers[2 * CHUNKS : 3 * CHUNKS])
    rows_of = buffers[3 * CHUNKS :]
    starts = [sum(widths[:k]) for k in range(CHUNKS)]
    section = lax.axis_index("sec")
    me = lax.axis_index("dev")
    bits = [(me // (1 << i)) % 2 for i in range(DIMS)]
    devices = {code: flipped(bits, mask_of(code)) for code in range(GROUP)}
    across = lax.rem(section + 2, 4)
    blocks, rows, halvings = plan.blocks, plan.rows, plan.halvings
    base = pl.ds(0, rows)
    owning = section < 3

    def peer(code):
        return (across if plan.core == 1 and code % 2 else section, devices[code])

    def when_owning(owns, run):
        if plan.core == 0:
            if owns:
                run()
        else:
            pl.when(owning if owns else jnp.logical_not(owning))(run)

    barrier = pltpu.get_barrier_semaphore()
    for code in range(1, GROUP):
        pl.semaphore_signal(barrier, inc=1, device_id=peer(code), device_id_type=MESH)
    pl.semaphore_wait(barrier, GROUP - 1)

    def passing(code):
        slot = code if plan.core == 0 else code // 2
        return pltpu.make_async_remote_copy(
            src_ref=latent_ref.at[devices[code]],
            dst_ref=latents.at[slot],
            send_sem=pass_send.at[code],
            recv_sem=pass_recv.at[slot],
            device_id=peer(code),
            device_id_type=MESH,
        )

    def pass_out():
        for code in range(1, GROUP):
            passing(code).start()
        latents[0] = latent_ref[me]

    def pass_in(codes):
        for code in codes:
            passing(code).wait_recv()

    when_owning(True, pass_out)
    if plan.core == 0:
        pass_in(range(1, GROUP))
    else:
        when_owning(True, lambda: pass_in(range(2, GROUP, 2)))
        when_owning(False, lambda: pass_in(range(1, GROUP, 2)))
    for head in range(2):
        lines = latents[pl.ds(0, blocks), head * ROWS : (head + 1) * ROWS, :].astype(jnp.float32)
        lines = lines.reshape(rows, lines.shape[2]).astype(jnp.bfloat16)
        valued = jnp.dot(lines, value_ref[head], preferred_element_type=jnp.float32)
        left[base, head * LANES : (head + 1) * LANES] = valued.astype(jnp.bfloat16)

    started = []

    def copy_of(source, target, phase, chunk, slot, out_slot, code):
        return pltpu.make_async_remote_copy(
            src_ref=source,
            dst_ref=target,
            send_sem=send_sem.at[phase, chunk, out_slot],
            recv_sem=recv_sem.at[phase, chunk, slot],
            device_id=peer(code),
            device_id_type=MESH,
        )

    def go(copy):
        copy.start()
        started.append(copy)
        return copy

    def halving(phase, chunk, step):
        half = (blocks // 2) >> step
        places = pl.ds(half, half)
        slot = 2 * SPREAD + step
        return copy_of(
            partial[chunk].at[places],
            landings[phase][chunk].at[places],
            phase,
            chunk,
            slot,
            slot,
            1 << plan.order(chunk)[step],
        )

    def direct(phase, chunk, place):
        return copy_of(
            partial[chunk].at[place],
            landings[phase][chunk].at[place],
            phase,
            chunk,
            place,
            place,
            plan.code(chunk, place),
        )

    def direct_across(phase, chunk, place):
        return copy_of(
            partial[chunk].at[place],
            landings[phase][chunk].at[16 + place],
            phase,
            chunk,
            SPREAD + place,
            SPREAD + place,
            plan.code(chunk, place) + 1,
        )

    def sum_send(phase, chunk, step):
        if step < halvings:
            go(halving(phase, chunk, step))
            return

        def to_owners():
            for place in range(1, SPREAD):
                direct(phase, chunk, place).start()

        def to_owners_across():
            for place in range(SPREAD):
                direct_across(phase, chunk, place).start()

        when_owning(True, to_owners)
        when_owning(False, to_owners_across)

    def sum_sent(phase):
        def to_owners():
            for chunk in range(CHUNKS):
                for place in range(1, SPREAD):
                    direct(phase, chunk, place).wait_send()

        def to_owners_across():
            for chunk in range(CHUNKS):
                for place in range(SPREAD):
                    direct_across(phase, chunk, place).wait_send()

        when_owning(True, to_owners)
        when_owning(False, to_owners_across)

    def all_sent():
        for copy in started:
            copy.wait_send()
        del started[:]

    def add_rows(phase, chunk, half, first, count):
        @pl.loop(0, count)
        def _(i):
            row = first + i
            partial[chunk][row] = partial[chunk][row] + landings[phase][chunk][half + row]

    def sum_step(phase, chunk, step):
        half = (blocks // 2) >> step
        halving(phase, chunk, step).wait_recv()
        ahead = half // 2 if step < halvings - 1 else 0
        add_rows(phase, chunk, half, ahead, half - ahead)
        sum_send(phase, chunk, step + 1)
        if ahead:
            add_rows(phase, chunk, half, 0, ahead)

    def sum_last(phase, chunk):
        total = partial[chunk][0].astype(jnp.float32)
        for place in range(1, SPREAD):
            direct(phase, chunk, place).wait_recv()
            total = total + landings[phase][chunk][place].astype(jnp.float32)
        if plan.core == 1:
            for place in range(SPREAD):
                direct_across(phase, chunk, place).wait_recv()
                total = total + landings[phase][chunk][16 + place].astype(jnp.float32)
        return total

    def tiled(chunk, one):
        whole = widths[chunk] // TILE

        @pl.loop(0, whole)
        def _(i):
            one(pl.multiple_of(i * TILE, TILE), TILE)

        if widths[chunk] % TILE:
            one(whole * TILE, widths[chunk] % TILE)

    def project(chunk, operand, weight, scale):
        def one(offset, size):
            inner = pl.ds(offset, size)
            outer = pl.ds(pl.multiple_of(starts[chunk] + offset, LANES), size)
            product = jnp.dot(
                operand[base, :], weight[:, outer], preferred_element_type=jnp.float32
            )
            if scale is not None:
                product = product * scale
            for i, code in enumerate(plan.codes()):
                block = product[i * ROWS : (i + 1) * ROWS]
                partial[chunk][plan.place(chunk, code), :, inner] = block.astype(jnp.bfloat16)

        tiled(chunk, one)

    loads[0].wait()
    for chunk in range(CHUNKS):
        project(chunk, left, out_weight, None)
        sum_send(0, chunk, 0)
    for step in range(halvings):
        for chunk in range(CHUNKS):
            sum_step(0, chunk, step)

    def gather_near(chunk, place):
        return copy_of(
            rows_of[chunk].at[0],
            rows_of[chunk].at[place],
            1,
            chunk,
            place,
            place,
            plan.code(chunk, place),
        )

    def gather_across(chunk, place):
        return copy_of(
            rows_of[chunk].at[0],
            rows_of[chunk].at[place],
            1,
            chunk,
            place,
            SPREAD + place,
            plan.code(chunk, place) + 1,
        )

    def doubling(chunk, step):
        count = (blocks // 2) >> step
        slot = 2 * SPREAD + step
        return copy_of(
            rows_of[chunk].at[pl.ds(0, count)],
            rows_of[chunk].at[pl.ds(count, count)],
            1,
            chunk,
            slot,
            slot,
            1 << plan.order(chunk)[step],
        )

    def attended_rows():
        square = jnp.zeros((ROWS, 1), jnp.float32)
        for chunk in range(CHUNKS):
            columns = pl.ds(starts[chunk], widths[chunk])
            total = residual_ref[:, columns].astype(jnp.float32) + sum_last(0, chunk)
            total = total.astype(jnp.bfloat16)
            stream[:, columns] = total
            total = total.astype(jnp.float32)
            square = square + jnp.sum(total * total, axis=1, keepdims=True)
            scaled = total * gain_ref[:, columns]
            rows_of[chunk][0, :, : widths[chunk]] = scaled.astype(jnp.bfloat16)
            if chunk == CHUNKS - 1:
                level = lax.rsqrt(square / stream.shape[1] + 1e-06)
                coarse = level.astype(jnp.bfloat16).astype(jnp.float32)
                lane = lax.broadcasted_iota(jnp.int32, (ROWS, LANES), 1)
                extra = share_ref[...].astype(jnp.float32)
                extra = jnp.where(lane == 2 * EXPERTS, coarse, extra)
                extra = jnp.where(lane == 2 * EXPERTS + 1, level - coarse, extra)
                rows_of[chunk][0, :, widths[chunk] :] = extra.astype(jnp.bfloat16)
            for place in range(SPREAD):
                if place:
                    gather_near(chunk, place).start()
                if plan.core == 1:
                    gather_across(chunk, place).start()

    when_owning(True, attended_rows)
    for step in reversed(range(halvings)):
        for chunk in range(CHUNKS):
            if step == halvings - 1:
                when_owning(False, lambda: gather_across(chunk, 0).wait_recv())
                for place in range(1, SPREAD):
                    gather_near(chunk, place).wait_recv()
            else:
                doubling(chunk, step + 1).wait_recv()
            go(doubling(chunk, step))
    gate_sum[base, :] = jnp.zeros((rows, gate_sum.shape[1]), jnp.float32)
    up_sum[base, :] = jnp.zeros((rows, up_sum.shape[1]), jnp.float32)
    loads[1].wait()
    loads[2].wait()

    def stacked(chunk, columns):
        lines = [
            rows_of[chunk][plan.place(chunk, code), :, columns].astype(jnp.float32)
            for code in plan.codes()
        ]
        return jnp.concatenate(lines, axis=0)

    for chunk in range(CHUNKS):
        doubling(chunk, 0).wait_recv()

        def one(offset, size):
            outer = pl.ds(pl.multiple_of(starts[chunk] + offset, LANES), size)
            lines = stacked(chunk, pl.ds(offset, size)).astype(jnp.bfloat16)
            gate_sum[base, :] += jnp.dot(lines, gate[outer, :], preferred_element_type=jnp.float32)
            up_sum[base, :] += jnp.dot(lines, up[outer, :], preferred_element_type=jnp.float32)

        tiled(chunk, one)

    shares = stacked(CHUNKS - 1, pl.ds(widths[CHUNKS - 1], LANES))
    lane = lax.broadcasted_iota(jnp.int32, shares.shape, 1)
    expert = me // (GROUP // EXPERTS)

    def picked(first, second):
        chosen = (lane == first) | (lane == second)
        return jnp.sum(jnp.where(chosen, shares, 0.0), axis=1, keepdims=True)

    share = picked(expert, expert + EXPERTS)
    level = picked(2 * EXPERTS, 2 * EXPERTS + 1)
    hidden = gate_sum[base, :] * level
    hidden = hidden / (1.0 + jnp.exp(-hidden)) * (up_sum[base, :] * level)
    act[base, :] = hidden.astype(jnp.bfloat16)
    loads[3].wait()
    all_sent()
    sum_sent(0)
    for chunk in range(CHUNKS):
        project(chunk, act, down, share)
        sum_send(2, chunk, 0)
    for step in range(halvings):
        for chunk in range(CHUNKS):
            sum_step(2, chunk, step)

    def finish():
        for chunk in range(CHUNKS):
            columns = pl.ds(starts[chunk], widths[chunk])
            result = stream[:, columns].astype(jnp.float32) + sum_last(2, chunk)
            out_ref[:, columns] = result.astype(jnp.bfloat16)
        for code in range(1, GROUP):
            passing(code).wait_send()
        for chunk in range(CHUNKS):
            for place in range(SPREAD):
                if place:
                    gather_near(chunk, place).wait_send()
                if plan.core == 1:
                    gather_across(chunk, place).wait_send()

    def blank():
        out_ref[...] = jnp.zeros_like(out_ref)

    when_owning(True, finish)
    when_owning(False, blank)
    all_sent()
    sum_sent(2)


def layer_kernel(
    widths,
    latent_ref,
    residual_ref,
    gain_ref,
    share_ref,
    value_ref,
    out_weight_hbm,
    gate_hbm,
    up_hbm,
    down_hbm,
    out_ref,
    out_weight,
    gate,
    up,
    down,
    latents,
    left,
    stream,
    gate_sum,
    up_sum,
    act,
    load_sem,
    pass_send,
    pass_recv,
    send_sem,
    recv_sem,
    *buffers,
):
    loads = []
    for i, (source, target) in enumerate(
        ((out_weight_hbm, out_weight), (gate_hbm, gate), (up_hbm, up), (down_hbm, down))
    ):
        load = pltpu.make_async_copy(source, target, load_sem.at[i])
        load.start()
        loads.append(load)
    refs = (latent_ref, residual_ref, gain_ref, share_ref, value_ref, out_ref)
    refs += (out_weight, gate, up, down, latents, left, stream, gate_sum, up_sum, act)
    refs += (pass_send, pass_recv, send_sem, recv_sem)
    core = lax.axis_index("sec") % 2
    for number in range(2):
        pl.when(core == number)(
            functools.partial(work, Plan(number), widths, refs, buffers, loads)
        )


def chunk_widths(width):
    units = width // LANES
    return [LANES * (units // CHUNKS + (1 if k < units % CHUNKS else 0)) for k in range(CHUNKS)]


def layer_tail(latents, residual, gain, shares, value_up, *weights):
    width = residual.shape[1]
    widths = chunk_widths(width)
    hidden = weights[1].shape[1]
    bf16, f32 = jnp.bfloat16, jnp.float32
    vmem = pl.BlockSpec(memory_space=pltpu.VMEM)
    hbm = pl.BlockSpec(memory_space=pl.ANY)
    scratch = [pltpu.VMEM(weight.shape, bf16) for weight in weights]
    scratch += [
        pltpu.VMEM(latents.shape, bf16),
        pltpu.VMEM((GROUP * ROWS, 2 * LANES), bf16),
        pltpu.VMEM((ROWS, width), bf16),
        pltpu.VMEM((GROUP * ROWS, hidden), f32),
        pltpu.VMEM((GROUP * ROWS, hidden), f32),
        pltpu.VMEM((GROUP * ROWS, hidden), bf16),
        pltpu.SemaphoreType.DMA((4,)),
        pltpu.SemaphoreType.DMA((GROUP,)),
        pltpu.SemaphoreType.DMA((GROUP,)),
        pltpu.SemaphoreType.DMA((3, CHUNKS, SLOTS)),
        pltpu.SemaphoreType.DMA((3, CHUNKS, SLOTS)),
    ]
    scratch += [pltpu.VMEM((GROUP, ROWS, w), bf16) for w in widths] * 3
    extra = [0] * (CHUNKS - 1) + [LANES]
    scratch += [pltpu.VMEM((GROUP, ROWS, w + e), bf16) for w, e in zip(widths, extra)]
    return pl.pallas_call(
        functools.partial(layer_kernel, widths),
        out_shape=jax.ShapeDtypeStruct(residual.shape, bf16),
        in_specs=[vmem] * 5 + [hbm] * 4,
        out_specs=vmem,
        scratch_shapes=scratch,
        compiler_params=pltpu.CompilerParams(
            collective_id=0, has_side_effects=True, vmem_limit_bytes=56 * 1024 * 1024
        ),
    )(latents, residual, gain, shares, value_up, *weights)


def body(
    queries,
    latent_cache,
    cache_length,
    residual,
    norm_gain,
    value_up,
    out_weight,
    gate_weight,
    up_weight,
    down_weight,
    expert_index,
    gate_level,
):
    latent_width = value_up.shape[1]
    score_scale = (value_up.shape[2] + queries.shape[2] - latent_width) ** (-0.5)
    scores = (
        jnp.einsum("thc,tpc->thp", queries, latent_cache, preferred_element_type=jnp.float32)
        * score_scale
    )
    position = lax.broadcasted_iota(jnp.int32, (1, 1, latent_cache.shape[1]), 2)
    usable = position < cache_length[:, None, None]
    masked = jnp.where(usable, scores, -1e30)
    highest = jnp.max(masked, axis=2, keepdims=True)
    expos = jnp.where(usable, jnp.exp(masked - highest), 0.0)
    weights = (expos / jnp.sum(expos, axis=2, keepdims=True)).astype(jnp.bfloat16)
    latent_out = jnp.einsum(
        "thp,tpc->thc", weights, latent_cache, preferred_element_type=jnp.float32
    )[:, :, :latent_width].astype(jnp.bfloat16)
    tokens, heads = latent_out.shape[:2]
    latents = jnp.swapaxes(latent_out, 0, 1).reshape(GROUP, heads // GROUP * tokens, latent_width)

    levels = gate_level.astype(jnp.float32)
    mix = levels / jnp.sum(levels, axis=1, keepdims=True)
    named = expert_index[:, :, None] == jnp.arange(EXPERTS, dtype=jnp.int32)[None, None, :]
    share = jnp.sum(jnp.where(named, mix[:, :, None], 0.0), axis=1)
    coarse = share.astype(jnp.bfloat16)
    fine = (share - coarse.astype(jnp.float32)).astype(jnp.bfloat16)
    shares = jnp.pad(jnp.concatenate([coarse, fine], axis=1), ((0, 0), (0, 128 - 2 * EXPERTS)))
    return layer_tail(
        latents,
        residual,
        norm_gain.reshape(1, -1),
        shares,
        value_up,
        out_weight,
        gate_weight,
        up_weight,
        down_weight,
    )


def solution(mesh):
    placed = (
        P(("sec", "dev"), None, None),
        P(("sec", "dev"), None, None),
        P(("sec", "dev")),
        P(("sec", "dev"), None),
        P(),
        P("dev", None, None),
        P("dev", None),
        P(None, "dev"),
        P(None, "dev"),
        P("dev", None),
        P(("sec", "dev"), None),
        P(("sec", "dev"), None),
    )
    return jax.shard_map(
        body, mesh=mesh, in_specs=placed, out_specs=P(("sec", "dev"), None), check_vma=False
    )
```

time: 133 us -> 117 us (0.88)
  waiting for transfers between devices: 11.3 us -> 0 us
  starting transfers between devices: 9.34 us -> 0 us
  Pallas kernels: 93.4 us -> 99.3 us
    all_to_all x1 -> x0, waiting for transfers between devices: 11.3 us -> none  [body(): lax.all_to_all(latent_out, 'dev', split_axis=1, concat_axis=0, tiled=True)]
    all_to_all x1 -> x0, starting transfers between devices: 9.34 us -> none  [body(): lax.all_to_all(latent_out, 'dev', split_axis=1, concat_axis=0, tiled=True)]
    pallas_call x1, Pallas kernels: 93.4 us -> 99.3 us  [layer_tail(): pl.pallas_call(functools.partial(layer_kernel, widths), out_shape=jax.Sha...]
  transfers between devices with their start and end apart: 1 -> 0, of which waited for: 1 -> 0; matrix products, arithmetic and copies ran while one was open for 1% -> 0% of each run, Pallas kernels for 0% -> 0%
where the time goes in v2:
time: 117 us
  Pallas kernels  99.3 us (85%)
  matrix products  12.6 us (11%)
  local copies, waits for them, and re-layouts  3.17 us (3%)
  other arithmetic  1.5 us (1%)
    pallas_call x1, Pallas kernels, layer_tail(): pl.pallas_call(functools.partial(layer_kernel, widths), out_shape=jax.Sha...  99.3 us
    dot_general x1, matrix products, body(): jnp.einsum('thp,tpc->thc', weights, latent_cache, preferred_element_type=...  6.6 us
    sub x1, matrix products, body(): expos = jnp.where(usable, jnp.exp(masked - highest), 0.0)  6 us

profile of v2, /device:TPU:0, one launch (start us, length us, event | category | flops | bytes accessed | tf_op | source)
XLA Modules:
  0.0 116.7 jit_solution(5980746617930043997)
XLA Ops:
  0.0 0.0 copy-start
  0.0 0.8 iota_compare_fusion
  0.8 0.3 copy-done
  1.1 6.0 %fusion.13 = (f32[8,64]{1,0:T(8,128)S(1)}, f32[8,64,1024]{2,1,0:T(8,128)S(1)}) fusion(pred[8,1024]{1,0:T(8,128)(4,1)S(1)} %iota_compare_fusion, bf16[8,64,576]{2,1,0:T(8,128)(2,1)S(1)} %copy-done, bf16[8,1024,576]{1,2,0:T(8,128)(2,1)} %param.13), kind=kOutput, calls=%fused_computation.24 | convolution fusion | flops 606602240 | bytes 12134400 | tf_op jit(solution)/shard_map/sub | solution.py:551
  7.1 6.6 %fusion.2 = bf16[8,64,576]{2,1,0:T(8,128)(2,1)S(1)} fusion(bf16[8,1024,576]{1,2,0:T(8,128)(2,1)} %param.13, f32[8,64,1024]{2,1,0:T(8,128)S(1)} %get-tuple-element.6, f32[8,64]{1,0:T(8,128)S(1)} %get-tuple-element.5), kind=kOutput, calls=%fused_computation.5 | convolution fusion | flops 605028352 | bytes 12126208 | tf_op jit(solution)/shard_map/thp,tpc->thc/dot_general | solution.py:553
  13.7 0.0 copy-start.1
  13.7 0.0 copy-start.2
  13.8 1.1 copy.19
  14.9 0.0 copy-done.1
  14.9 0.0 copy-done.2
  14.9 0.1 copy.21
  15.0 0.1 copy.22
  15.1 0.7 fusion.10.share_ref
  15.8 99.3 %shard_map.118 = bf16[8,7168]{1,0:T(8,128)(2,1)} custom-call(bf16[32,16,512]{2,1,0:T(8,128)(2,1)} %bitcast.7, bf16[8,7168]{1,0:T(8,128)(2,1)} %residual_ref.1, f32[1,7168]{1,0:T(1,128)} %bitcast.8, bf16[8,128]{1,0:T(8,128)(2,1)} %fusion.10.share_ref, bf16[2,512,128]{2,1,0:T(8,128)(2,1)} %value_ref.1, bf16[256,7168]{1,0:T(8,128)(2,1)} %out_weight_hbm.1, ...), custom_call_target="tpu_custom_call" | custom-call | tf_op jit(solution)/shard_map/pallas_call | solution.py:515
  115.1 1.6 %copy.24 = bf16[8,7168]{1,0:T(8,128)(2,1)} copy(bf16[8,7168]{1,0:T(8,128)(2,1)} %shard_map.118) | data formatting | bytes 229376
  (6 shorter events, 0.1 us)
Async XLA Ops:
  0.0 1.1 copy-start
  13.7 1.2 copy-start.1
  13.7 1.2 %copy-start.2 = (s32[8,2]{0,1:T(2,128)S(1)}, s32[8,2]{0,1:T(2,128)}, u32[]{:S(2)}) copy-start(s32[8,2]{0,1:T(2,128)} %param.22) | copy-start | bytes 196

commit v3 on v2

--- a/solution.py
+++ b/solution.py
@@ -14,7 +14,20 @@
 DIMS = 5
 TILE = 256
 LANES = 128
-CHUNKS = 8
+TABLE = (
+    ((0, 1, 2, 3, 4), 0, 6),
+    ((1, 2, 3, 4, 0), 1, 6),
+    ((2, 3, 4, 0, 1), 2, 6),
+    ((3, 4, 0, 1, 2), 3, 6),
+    ((4, 0, 1, 2, 3), 0, 6),
+    ((0, 1, 2, 3, 4), 2, 6),
+    ((1, 2, 3, 4, 0), 3, 5),
+    ((2, 3, 4, 0, 1), 0, 5),
+    ((3, 4, 0, 1, 2), 1, 5),
+    ((4, 0, 1, 2, 3), 1, 5),
+)
+LAG = 0
+CHUNKS = len(TABLE)
 SPREAD = 4
 SLOTS = 2 * SPREAD + 3
 MASKS = (1, 2, 6, 8, 24)
@@ -44,11 +57,9 @@
         self.rows = self.blocks * ROWS
 
     def order(self, chunk):
-        turn = chunk // 2 if self.core == 0 else chunk
-        ring = [1 + (turn + i) % 4 for i in range(4)]
-        if self.core == 1:
-            return ring
-        return [0] + ring if chunk % 2 == 0 else ring + [0]
+        if self.core == 0:
+            return TABLE[chunk][0]
+        return [1 + (TABLE[chunk][1] + i) % 4 for i in range(4)]
 
     def codes(self):
         return [(code if self.core == 0 else 2 * code) for code in range(self.blocks)]
@@ -66,6 +77,67 @@
         for step, dim in enumerate(order):
             code += ((place >> (len(order) - 1 - step)) & 1) << dim
         return code
+
+
+def places():
+    section = lax.axis_index("sec")
+    me = lax.axis_index("dev")
+    bits = [(me // (1 << i)) % 2 for i in range(DIMS)]
+    devices = {code: flipped(bits, mask_of(code)) for code in range(GROUP)}
+    return section, me, devices
+
+
+def partner(plan, section, devices, code):
+    across = lax.rem(section + 2, 4)
+    return (across if plan.core == 1 and code % 2 else section, devices[code])
+
+
+def greet(plan):
+    section, _, devices = places()
+    barrier = pltpu.get_barrier_semaphore()
+    for code in range(1, GROUP):
+        pl.semaphore_signal(
+            barrier,
+            inc=1,
+            device_id=partner(plan, section, devices, code),
+            device_id_type=MESH,
+        )
+
+
+def attend(query_ref, length_ref, cache_hbm, cache, by_head, latent_ref, cache_sem, start_loads):
+    tokens, heads, _ = query_ref.shape
+    latent_width = LANES * len(by_head)
+    value_width = LANES
+    score_scale = (value_width + query_ref.shape[2] - latent_width) ** (-0.5)
+    fetches = []
+    for token in range(tokens):
+        fetch = pltpu.make_async_copy(cache_hbm.at[token], cache.at[token], cache_sem.at[token])
+        fetch.start()
+        fetches.append(fetch)
+    position = lax.broadcasted_iota(jnp.int32, (heads, cache.shape[2]), 1)
+    for token in range(tokens):
+        fetches[token].wait()
+        if token == 2:
+            start_loads()
+        scores = jnp.dot(query_ref[token], cache[token], preferred_element_type=jnp.float32)
+        usable = position < length_ref[token]
+        masked = jnp.where(usable, scores * score_scale, -1e30)
+        highest = jnp.max(masked, axis=1, keepdims=True)
+        expos = jnp.where(usable, jnp.exp(masked - highest), 0.0)
+        weights = expos * (1.0 / jnp.sum(expos, axis=1, keepdims=True))
+        mixed = lax.dot_general(
+            weights.astype(jnp.bfloat16),
+            cache[token, 0:latent_width, :],
+            (((1,), (1,)), ((), ())),
+            preferred_element_type=jnp.float32,
+        )
+        for part, lines in enumerate(by_head):
+            columns = slice(part * LANES, (part + 1) * LANES)
+            lines[pl.ds(token, heads, stride=tokens), :] = mixed[:, columns]
+    dests, rows, _ = latent_ref.shape
+    for part, lines in enumerate(by_head):
+        columns = slice(part * LANES, (part + 1) * LANES)
+        latent_ref[:, :, columns] = lines[...].reshape(dests, rows, LANES).astype(jnp.bfloat16)
 
 
 def work(plan, widths, refs, buffers, loads):
@@ -83,6 +155,7 @@
         latents,
         left,
         stream,
+        square,
         gate_sum,
         up_sum,
         act,
@@ -95,17 +168,13 @@
     landings = (buffers[CHUNKS : 2 * CHUNKS], None, buffers[2 * CHUNKS : 3 * CHUNKS])
     rows_of = buffers[3 * CHUNKS :]
     starts = [sum(widths[:k]) for k in range(CHUNKS)]
-    section = lax.axis_index("sec")
-    me = lax.axis_index("dev")
-    bits = [(me // (1 << i)) % 2 for i in range(DIMS)]
-    devices = {code: flipped(bits, mask_of(code)) for code in range(GROUP)}
-    across = lax.rem(section + 2, 4)
+    section, me, devices = places()
     blocks, rows, halvings = plan.blocks, plan.rows, plan.halvings
     base = pl.ds(0, rows)
     owning = section < 3
 
     def peer(code):
-        return (across if plan.core == 1 and code % 2 else section, devices[code])
+        return partner(plan, section, devices, code)
 
     def when_owning(owns, run):
         if plan.core == 0:
@@ -114,10 +183,7 @@
         else:
             pl.when(owning if owns else jnp.logical_not(owning))(run)
 
-    barrier = pltpu.get_barrier_semaphore()
-    for code in range(1, GROUP):
-        pl.semaphore_signal(barrier, inc=1, device_id=peer(code), device_id_type=MESH)
-    pl.semaphore_wait(barrier, GROUP - 1)
+    pl.semaphore_wait(pltpu.get_barrier_semaphore(), GROUP - 1)
 
     def passing(code):
         slot = code if plan.core == 0 else code // 2
@@ -290,14 +356,6 @@
 
         tiled(chunk, one)
 
-    loads[0].wait()
-    for chunk in range(CHUNKS):
-        project(chunk, left, out_weight, None)
-        sum_send(0, chunk, 0)
-    for step in range(halvings):
-        for chunk in range(CHUNKS):
-            sum_step(0, chunk, step)
-
     def gather_near(chunk, place):
         return copy_of(
             rows_of[chunk].at[0],
@@ -333,45 +391,37 @@
             1 << plan.order(chunk)[step],
         )
 
-    def attended_rows():
-        square = jnp.zeros((ROWS, 1), jnp.float32)
-        for chunk in range(CHUNKS):
-            columns = pl.ds(starts[chunk], widths[chunk])
-            total = residual_ref[:, columns].astype(jnp.float32) + sum_last(0, chunk)
-            total = total.astype(jnp.bfloat16)
-            stream[:, columns] = total
-            total = total.astype(jnp.float32)
-            square = square + jnp.sum(total * total, axis=1, keepdims=True)
-            scaled = total * gain_ref[:, columns]
-            rows_of[chunk][0, :, : widths[chunk]] = scaled.astype(jnp.bfloat16)
-            if chunk == CHUNKS - 1:
-                level = lax.rsqrt(square / stream.shape[1] + 1e-06)
-                coarse = level.astype(jnp.bfloat16).astype(jnp.float32)
-                lane = lax.broadcasted_iota(jnp.int32, (ROWS, LANES), 1)
-                extra = share_ref[...].astype(jnp.float32)
-                extra = jnp.where(lane == 2 * EXPERTS, coarse, extra)
-                extra = jnp.where(lane == 2 * EXPERTS + 1, level - coarse, extra)
-                rows_of[chunk][0, :, widths[chunk] :] = extra.astype(jnp.bfloat16)
-            for place in range(SPREAD):
-                if place:
-                    gather_near(chunk, place).start()
-                if plan.core == 1:
-                    gather_across(chunk, place).start()
-
-    when_owning(True, attended_rows)
-    for step in reversed(range(halvings)):
-        for chunk in range(CHUNKS):
-            if step == halvings - 1:
-                when_owning(False, lambda: gather_across(chunk, 0).wait_recv())
-                for place in range(1, SPREAD):
-                    gather_near(chunk, place).wait_recv()
-            else:
-                doubling(chunk, step + 1).wait_recv()
-            go(doubling(chunk, step))
-    gate_sum[base, :] = jnp.zeros((rows, gate_sum.shape[1]), jnp.float32)
-    up_sum[base, :] = jnp.zeros((rows, up_sum.shape[1]), jnp.float32)
-    loads[1].wait()
-    loads[2].wait()
+    def attended_rows(chunk):
+        columns = pl.ds(starts[chunk], widths[chunk])
+        total = residual_ref[:, columns].astype(jnp.float32) + sum_last(0, chunk)
+        total = total.astype(jnp.bfloat16)
+        stream[:, columns] = total
+        total = total.astype(jnp.float32)
+        squares = total * total
+        folded = sum(squares[:, i : i + LANES] for i in range(0, widths[chunk], LANES))
+        square[...] = folded if chunk == 0 else square[...] + folded
+        scaled = total * gain_ref[:, columns]
+        rows_of[chunk][0, :, : widths[chunk]] = scaled.astype(jnp.bfloat16)
+        if chunk == CHUNKS - 1:
+            mean = jnp.sum(square[...], axis=1, keepdims=True) / stream.shape[1]
+            level = lax.rsqrt(mean + 1e-06)
+            coarse = level.astype(jnp.bfloat16).astype(jnp.float32)
+            lane = lax.broadcasted_iota(jnp.int32, (ROWS, LANES), 1)
+            extra = share_ref[...].astype(jnp.float32)
+            extra = jnp.where(lane == 2 * EXPERTS, coarse, extra)
+            extra = jnp.where(lane == 2 * EXPERTS + 1, level - coarse, extra)
+            rows_of[chunk][0, :, widths[chunk] :] = extra.astype(jnp.bfloat16)
+        for place in range(SPREAD):
+            if place:
+                gather_near(chunk, place).start()
+            if plan.core == 1:
+                gather_across(chunk, place).start()
+
+    def first_doubling(chunk):
+        when_owning(False, lambda: gather_across(chunk, 0).wait_recv())
+        for place in range(1, SPREAD):
+            gather_near(chunk, place).wait_recv()
+        go(doubling(chunk, halvings - 1))
 
     def stacked(chunk, columns):
         lines = [
@@ -380,7 +430,7 @@
         ]
         return jnp.concatenate(lines, axis=0)
 
-    for chunk in range(CHUNKS):
+    def hidden_sums(chunk):
         doubling(chunk, 0).wait_recv()
 
         def one(offset, size):
@@ -391,6 +441,49 @@
 
         tiled(chunk, one)
 
+    def staggered(count, stage):
+        for time in range(count + LAG * (CHUNKS // DIMS - 1)):
+            for group in range(CHUNKS // DIMS):
+                if 0 <= time - LAG * group < count:
+                    for chunk in range(group * DIMS, (group + 1) * DIMS):
+                        stage(chunk, time - LAG * group)
+
+    def until_hidden(chunk, step):
+        if step == 0:
+            project(chunk, left, out_weight, None)
+            sum_send(0, chunk, 0)
+        elif step <= halvings:
+            sum_step(0, chunk, step - 1)
+        elif step == halvings + 1:
+            when_owning(True, functools.partial(attended_rows, chunk))
+        elif step == halvings + 2:
+            first_doubling(chunk)
+        elif step <= 2 * halvings + 1:
+            done = step - halvings - 2
+            doubling(chunk, halvings - done).wait_recv()
+            go(doubling(chunk, halvings - done - 1))
+        else:
+            hidden_sums(chunk)
+
+    def until_output(chunk, step):
+        if step == 0:
+            project(chunk, act, down, share)
+            sum_send(2, chunk, 0)
+        elif step <= halvings:
+            sum_step(2, chunk, step - 1)
+        else:
+            when_owning(True, functools.partial(result_rows, chunk))
+
+    def result_rows(chunk):
+        columns = pl.ds(starts[chunk], widths[chunk])
+        result = stream[:, columns].astype(jnp.float32) + sum_last(2, chunk)
+        out_ref[:, columns] = result.astype(jnp.bfloat16)
+
+    gate_sum[base, :] = jnp.zeros((rows, gate_sum.shape[1]), jnp.float32)
+    up_sum[base, :] = jnp.zeros((rows, up_sum.shape[1]), jnp.float32)
+    for load in loads[:3]:
+        load.wait()
+    staggered(2 * halvings + 3, until_hidden)
     shares = stacked(CHUNKS - 1, pl.ds(widths[CHUNKS - 1], LANES))
     lane = lax.broadcasted_iota(jnp.int32, shares.shape, 1)
     expert = me // (GROUP // EXPERTS)
@@ -407,18 +500,9 @@
     loads[3].wait()
     all_sent()
     sum_sent(0)
-    for chunk in range(CHUNKS):
-        project(chunk, act, down, share)
-        sum_send(2, chunk, 0)
-    for step in range(halvings):
-        for chunk in range(CHUNKS):
-            sum_step(2, chunk, step)
+    staggered(halvings + 2, until_output)
 
     def finish():
-        for chunk in range(CHUNKS):
-            columns = pl.ds(starts[chunk], widths[chunk])
-            result = stream[:, columns].astype(jnp.float32) + sum_last(2, chunk)
-            out_ref[:, columns] = result.astype(jnp.bfloat16)
         for code in range(1, GROUP):
             passing(code).wait_send()
         for chunk in range(CHUNKS):
@@ -439,11 +523,13 @@
 
 def layer_kernel(
     widths,
-    latent_ref,
+    length_ref,
+    query_ref,
     residual_ref,
     gain_ref,
     share_ref,
     value_ref,
+    cache_hbm,
     out_weight_hbm,
     gate_hbm,
     up_hbm,
@@ -453,12 +539,16 @@
     gate,
     up,
     down,
+    cache,
+    latent_ref,
     latents,
     left,
     stream,
+    square,
     gate_sum,
     up_sum,
     act,
+    cache_sem,
     load_sem,
     pass_send,
     pass_recv,
@@ -466,62 +556,80 @@
     recv_sem,
     *buffers,
 ):
-    loads = []
-    for i, (source, target) in enumerate(
-        ((out_weight_hbm, out_weight), (gate_hbm, gate), (up_hbm, up), (down_hbm, down))
-    ):
-        load = pltpu.make_async_copy(source, target, load_sem.at[i])
-        load.start()
-        loads.append(load)
+    parts = latent_ref.shape[2] // LANES
+    by_head, buffers = buffers[:parts], buffers[parts:]
+    loads = [
+        pltpu.make_async_copy(source, target, load_sem.at[i])
+        for i, (source, target) in enumerate(
+            ((out_weight_hbm, out_weight), (gate_hbm, gate), (up_hbm, up), (down_hbm, down))
+        )
+    ]
     refs = (latent_ref, residual_ref, gain_ref, share_ref, value_ref, out_ref)
-    refs += (out_weight, gate, up, down, latents, left, stream, gate_sum, up_sum, act)
+    refs += (out_weight, gate, up, down, latents, left, stream, square, gate_sum, up_sum, act)
     refs += (pass_send, pass_recv, send_sem, recv_sem)
-    core = lax.axis_index("sec") % 2
+    section = lax.axis_index("sec")
+    core = section % 2
+    for number in range(2):
+        pl.when(core == number)(functools.partial(greet, Plan(number)))
+
+    def start_loads():
+        for load in loads:
+            load.start()
+
+    pl.when(section < 3)(
+        lambda: attend(
+            query_ref, length_ref, cache_hbm, cache, by_head, latent_ref, cache_sem, start_loads
+        )
+    )
+    pl.when(section == 3)(start_loads)
     for number in range(2):
         pl.when(core == number)(
             functools.partial(work, Plan(number), widths, refs, buffers, loads)
         )
 
 
-def chunk_widths(width):
-    units = width // LANES
-    return [LANES * (units // CHUNKS + (1 if k < units % CHUNKS else 0)) for k in range(CHUNKS)]
-
-
-def layer_tail(latents, residual, gain, shares, value_up, *weights):
+def layer(lengths, queries, residual, gain, shares, value_up, cache, *weights):
     width = residual.shape[1]
-    widths = chunk_widths(width)
+    widths = [LANES * units for _, _, units in TABLE]
     hidden = weights[1].shape[1]
+    tokens, heads, _ = queries.shape
+    latent_width = value_up.shape[1]
     bf16, f32 = jnp.bfloat16, jnp.float32
     vmem = pl.BlockSpec(memory_space=pltpu.VMEM)
     hbm = pl.BlockSpec(memory_space=pl.ANY)
+    latents = pltpu.VMEM((GROUP, heads * tokens // GROUP, latent_width), bf16)
     scratch = [pltpu.VMEM(weight.shape, bf16) for weight in weights]
     scratch += [
-        pltpu.VMEM(latents.shape, bf16),
+        pltpu.VMEM(cache.shape, bf16),
+        latents,
+        latents,
         pltpu.VMEM((GROUP * ROWS, 2 * LANES), bf16),
         pltpu.VMEM((ROWS, width), bf16),
+        pltpu.VMEM((ROWS, LANES), f32),
         pltpu.VMEM((GROUP * ROWS, hidden), f32),
         pltpu.VMEM((GROUP * ROWS, hidden), f32),
         pltpu.VMEM((GROUP * ROWS, hidden), bf16),
+        pltpu.SemaphoreType.DMA((tokens,)),
         pltpu.SemaphoreType.DMA((4,)),
         pltpu.SemaphoreType.DMA((GROUP,)),
         pltpu.SemaphoreType.DMA((GROUP,)),
         pltpu.SemaphoreType.DMA((3, CHUNKS, SLOTS)),
         pltpu.SemaphoreType.DMA((3, CHUNKS, SLOTS)),
     ]
+    scratch += [pltpu.VMEM((heads * tokens, LANES), f32)] * (latent_width // LANES)
     scratch += [pltpu.VMEM((GROUP, ROWS, w), bf16) for w in widths] * 3
     extra = [0] * (CHUNKS - 1) + [LANES]
     scratch += [pltpu.VMEM((GROUP, ROWS, w + e), bf16) for w, e in zip(widths, extra)]
     return pl.pallas_call(
         functools.partial(layer_kernel, widths),
         out_shape=jax.ShapeDtypeStruct(residual.shape, bf16),
-        in_specs=[vmem] * 5 + [hbm] * 4,
+        in_specs=[pl.BlockSpec(memory_space=pltpu.SMEM)] + [vmem] * 5 + [hbm] * 5,
         out_specs=vmem,
         scratch_shapes=scratch,
         compiler_params=pltpu.CompilerParams(
-            collective_id=0, has_side_effects=True, vmem_limit_bytes=56 * 1024 * 1024
+            collective_id=0, has_side_effects=True, vmem_limit_bytes=58 * 1024 * 1024
         ),
-    )(latents, residual, gain, shares, value_up, *weights)
+    )(lengths, queries, residual, gain, shares, value_up, cache, *weights)
 
 
 def body(
@@ -538,24 +646,6 @@
     expert_index,
     gate_level,
 ):
-    latent_width = value_up.shape[1]
-    score_scale = (value_up.shape[2] + queries.shape[2] - latent_width) ** (-0.5)
-    scores = (
-        jnp.einsum("thc,tpc->thp", queries, latent_cache, preferred_element_type=jnp.float32)
-        * score_scale
-    )
-    position = lax.broadcasted_iota(jnp.int32, (1, 1, latent_cache.shape[1]), 2)
-    usable = position < cache_length[:, None, None]
-    masked = jnp.where(usable, scores, -1e30)
-    highest = jnp.max(masked, axis=2, keepdims=True)
-    expos = jnp.where(usable, jnp.exp(masked - highest), 0.0)
-    weights = (expos / jnp.sum(expos, axis=2, keepdims=True)).astype(jnp.bfloat16)
-    latent_out = jnp.einsum(
-        "thp,tpc->thc", weights, latent_cache, preferred_element_type=jnp.float32
-    )[:, :, :latent_width].astype(jnp.bfloat16)
-    tokens, heads = latent_out.shape[:2]
-    latents = jnp.swapaxes(latent_out, 0, 1).reshape(GROUP, heads // GROUP * tokens, latent_width)
-
     levels = gate_level.astype(jnp.float32)
     mix = levels / jnp.sum(levels, axis=1, keepdims=True)
     named = expert_index[:, :, None] == jnp.arange(EXPERTS, dtype=jnp.int32)[None, None, :]
@@ -563,12 +653,14 @@
     coarse = share.astype(jnp.bfloat16)
     fine = (share - coarse.astype(jnp.float32)).astype(jnp.bfloat16)
     shares = jnp.pad(jnp.concatenate([coarse, fine], axis=1), ((0, 0), (0, 128 - 2 * EXPERTS)))
-    return layer_tail(
-        latents,
+    return layer(
+        cache_length,
+        queries,
         residual,
         norm_gain.reshape(1, -1),
         shares,
         value_up,
+        jnp.swapaxes(latent_cache, 1, 2),
         out_weight,
         gate_weight,
         up_weight,

time: 117 us -> 101 us (0.86)
  matrix products: 12.6 us -> 0 us
  Pallas kernels: 99.3 us -> 96.8 us
  local copies, waits for them, and re-layouts: 3.17 us -> 1.73 us
  other arithmetic: 1.5 us -> 2.74 us
    dot_general x1 -> x0, matrix products: 6.6 us -> none  [body(): jnp.einsum('thp,tpc->thc', weights, latent_cache, preferred_element_type=...]
    sub x1 -> x0, matrix products: 6 us -> none  [body(): expos = jnp.where(usable, jnp.exp(masked - highest), 0.0)]
    pallas_call x1, Pallas kernels: 99.3 us -> 96.8 us  [layer(): pl.pallas_call(functools.partial(layer_kernel, widths), out_shape=jax.Sha...]
where the time goes in v3:
time: 101 us
  Pallas kernels  96.8 us (96%)
  other arithmetic  2.74 us (3%)
  local copies, waits for them, and re-layouts  1.73 us (2%)
    pallas_call x1, Pallas kernels, layer(): pl.pallas_call(functools.partial(layer_kernel, widths), out_shape=jax.Sha...  96.8 us

profile of v3, /device:TPU:0, one launch (start us, length us, event | category | flops | bytes accessed | tf_op | source)
XLA Modules:
  0.0 101.3 jit_solution(9682575448925227714)
XLA Ops:
  0.0 0.7 convert_reduce_fusion
  0.7 0.7 convert_divide_fusion
  1.4 0.7 select_reduce_fusion
  2.1 0.1 copy.19
  2.2 0.1 copy.18
  2.3 0.7 fusion.2.share_ref
  2.9 96.8 %shard_map.118 = bf16[8,7168]{1,0:T(8,128)(2,1)} custom-call(s32[8]{0:T(128)} %length_ref.1, bf16[8,64,576]{2,1,0:T(8,128)(2,1)} %query_ref.1, bf16[8,7168]{1,0:T(8,128)(2,1)} %residual_ref.1, f32[1,7168]{1,0:T(1,128)} %bitcast.3, bf16[8,128]{1,0:T(8,128)(2,1)} %fusion.2.share_ref, bf16[2,512,128]{2,1,0:T(8,128)(2,1)} %value_ref.1, ...), custom_call_target="tpu_custom_call" | custom-call | tf_op jit(solution)/shard_map/pallas_call | solution.py:623
  99.7 1.6 %copy.21 = bf16[8,7168]{1,0:T(8,128)(2,1)} copy(bf16[8,7168]{1,0:T(8,128)(2,1)} %shard_map.118) | data formatting | bytes 229376
  (2 shorter events, 0.0 us)

commit v4 on v3

--- a/solution.py
+++ b/solution.py
@@ -29,7 +29,8 @@
 LAG = 0
 CHUNKS = len(TABLE)
 SPREAD = 4
-SLOTS = 2 * SPREAD + 3
+NEAR, FAR, HALVED = 0, 1, 2
+SLOTS = HALVED + 3
 MASKS = (1, 2, 6, 8, 24)
 MESH = pl.DeviceIdType.MESH
 
@@ -145,7 +146,8 @@
         latent_ref,
         residual_ref,
         gain_ref,
-        share_ref,
+        expert_ref,
+        level_ref,
         value_ref,
         out_ref,
         out_weight,
@@ -190,9 +192,19 @@
         return pltpu.make_async_remote_copy(
             src_ref=latent_ref.at[devices[code]],
             dst_ref=latents.at[slot],
-            send_sem=pass_send.at[code],
-            recv_sem=pass_recv.at[slot],
+            send_sem=pass_send,
+            recv_sem=pass_recv,
             device_id=peer(code),
+            device_id_type=MESH,
+        )
+
+    def passed(slots):
+        return pltpu.make_async_remote_copy(
+            src_ref=latent_ref.at[slots],
+            dst_ref=latents.at[slots],
+            send_sem=pass_send,
+            recv_sem=pass_recv,
+            device_id=peer(1),
             device_id_type=MESH,
         )
 
@@ -200,110 +212,80 @@
         for code in range(1, GROUP):
             passing(code).start()
         latents[0] = latent_ref[me]
-
-    def pass_in(codes):
-        for code in codes:
-            passing(code).wait_recv()
+        passed(pl.ds(1, blocks - 1)).wait_recv()
 
     when_owning(True, pass_out)
-    if plan.core == 0:
-        pass_in(range(1, GROUP))
-    else:
-        when_owning(True, lambda: pass_in(range(2, GROUP, 2)))
-        when_owning(False, lambda: pass_in(range(1, GROUP, 2)))
+    when_owning(False, lambda: passed(pl.ds(0, blocks)).wait_recv())
     for head in range(2):
         lines = latents[pl.ds(0, blocks), head * ROWS : (head + 1) * ROWS, :].astype(jnp.float32)
         lines = lines.reshape(rows, lines.shape[2]).astype(jnp.bfloat16)
         valued = jnp.dot(lines, value_ref[head], preferred_element_type=jnp.float32)
         left[base, head * LANES : (head + 1) * LANES] = valued.astype(jnp.bfloat16)
 
-    started = []
-
-    def copy_of(source, target, phase, chunk, slot, out_slot, code):
+    def copy_of(source, target, phase, chunk, slot, code):
         return pltpu.make_async_remote_copy(
             src_ref=source,
             dst_ref=target,
-            send_sem=send_sem.at[phase, chunk, out_slot],
-            recv_sem=recv_sem.at[phase, chunk, slot],
+            send_sem=send_sem.at[phase % 2, chunk],
+            recv_sem=recv_sem.at[phase % 2, chunk, slot],
             device_id=peer(code),
             device_id_type=MESH,
         )
 
-    def go(copy):
-        copy.start()
-        started.append(copy)
-        return copy
+    def arrived(buffer, places, phase, chunk, slot):
+        lines = buffer[chunk].at[places]
+        copy_of(lines, lines, phase, chunk, slot, 1).wait_recv()
+
+    def sent(buffer, phase, count):
+        for chunk in range(CHUNKS):
+            lines = buffer[chunk].at[pl.ds(0, count)]
+            copy_of(lines, lines, phase, chunk, NEAR, 1).wait_send()
 
     def halving(phase, chunk, step):
         half = (blocks // 2) >> step
         places = pl.ds(half, half)
-        slot = 2 * SPREAD + step
         return copy_of(
             partial[chunk].at[places],
             landings[phase][chunk].at[places],
             phase,
             chunk,
-            slot,
-            slot,
+            HALVED + step,
             1 << plan.order(chunk)[step],
-        )
-
-    def direct(phase, chunk, place):
-        return copy_of(
-            partial[chunk].at[place],
-            landings[phase][chunk].at[place],
-            phase,
-            chunk,
-            place,
-            place,
-            plan.code(chunk, place),
-        )
-
-    def direct_across(phase, chunk, place):
-        return copy_of(
-            partial[chunk].at[place],
-            landings[phase][chunk].at[16 + place],
-            phase,
-            chunk,
-            SPREAD + place,
-            SPREAD + place,
-            plan.code(chunk, place) + 1,
         )
 
     def sum_send(phase, chunk, step):
         if step < halvings:
-            go(halving(phase, chunk, step))
+            halving(phase, chunk, step).start()
             return
 
         def to_owners():
             for place in range(1, SPREAD):
-                direct(phase, chunk, place).start()
+                copy_of(
+                    partial[chunk].at[place],
+                    landings[phase][chunk].at[place],
+                    phase,
+                    chunk,
+                    NEAR,
+                    plan.code(chunk, place),
+                ).start()
 
         def to_owners_across():
             for place in range(SPREAD):
-                direct_across(phase, chunk, place).start()
+                copy_of(
+                    partial[chunk].at[place],
+                    landings[phase][chunk].at[16 + place],
+                    phase,
+                    chunk,
+                    FAR,
+                    plan.code(chunk, place) + 1,
+                ).start()
 
         when_owning(True, to_owners)
         when_owning(False, to_owners_across)
 
     def sum_sent(phase):
-        def to_owners():
-            for chunk in range(CHUNKS):
-                for place in range(1, SPREAD):
-                    direct(phase, chunk, place).wait_send()
-
-        def to_owners_across():
-            for chunk in range(CHUNKS):
-                for place in range(SPREAD):
-                    direct_across(phase, chunk, place).wait_send()
-
-        when_owning(True, to_owners)
-        when_owning(False, to_owners_across)
-
-    def all_sent():
-        for copy in started:
-            copy.wait_send()
-        del started[:]
+        when_owning(True, lambda: sent(partial, phase, blocks - 1))
+        when_owning(False, lambda: sent(partial, phase, blocks))
 
     def add_rows(phase, chunk, half, first, count):
         @pl.loop(0, count)
@@ -322,12 +304,12 @@
 
     def sum_last(phase, chunk):
         total = partial[chunk][0].astype(jnp.float32)
+        arrived(landings[phase], pl.ds(1, SPREAD - 1), phase, chunk, NEAR)
         for place in range(1, SPREAD):
-            direct(phase, chunk, place).wait_recv()
             total = total + landings[phase][chunk][place].astype(jnp.float32)
         if plan.core == 1:
+            arrived(landings[phase], pl.ds(16, SPREAD), phase, chunk, FAR)
             for place in range(SPREAD):
-                direct_across(phase, chunk, place).wait_recv()
                 total = total + landings[phase][chunk][16 + place].astype(jnp.float32)
         return total
 
@@ -356,40 +338,44 @@
 
         tiled(chunk, one)
 
-    def gather_near(chunk, place):
+    def gather(chunk, place, across):
         return copy_of(
             rows_of[chunk].at[0],
             rows_of[chunk].at[place],
             1,
             chunk,
-            place,
-            place,
-            plan.code(chunk, place),
-        )
-
-    def gather_across(chunk, place):
-        return copy_of(
-            rows_of[chunk].at[0],
-            rows_of[chunk].at[place],
-            1,
-            chunk,
-            place,
-            SPREAD + place,
-            plan.code(chunk, place) + 1,
+            NEAR,
+            plan.code(chunk, place) + across,
         )
 
     def doubling(chunk, step):
         count = (blocks // 2) >> step
-        slot = 2 * SPREAD + step
         return copy_of(
             rows_of[chunk].at[pl.ds(0, count)],
             rows_of[chunk].at[pl.ds(count, count)],
             1,
             chunk,
-            slot,
-            slot,
+            HALVED + step,
             1 << plan.order(chunk)[step],
         )
+
+    def share_lanes():
+        lane = lax.broadcasted_iota(jnp.int32, (ROWS, LANES), 1)
+        own = lax.broadcasted_iota(jnp.int32, (ROWS, ROWS), 0) == lax.broadcasted_iota(
+            jnp.int32, (ROWS, ROWS), 1
+        )
+
+        def column(ref, k):
+            line = jnp.broadcast_to(ref[k : k + 1, :].astype(jnp.float32), (ROWS, ROWS))
+            return jnp.sum(jnp.where(own, line, 0.0), axis=1, keepdims=True)
+
+        levels = [column(level_ref, k) for k in range(TOPK)]
+        named = jnp.where(lane < EXPERTS, lane, lane - EXPERTS).astype(jnp.float32)
+        mixed = jnp.zeros((ROWS, LANES), jnp.float32)
+        for k in range(TOPK):
+            mixed += jnp.where(named == column(expert_ref, k), levels[k] / sum(levels), 0.0)
+        coarse = mixed.astype(jnp.bfloat16).astype(jnp.float32)
+        return lane, jnp.where(lane < EXPERTS, coarse, mixed - coarse)
 
     def attended_rows(chunk):
         columns = pl.ds(starts[chunk], widths[chunk])
@@ -406,22 +392,20 @@
             mean = jnp.sum(square[...], axis=1, keepdims=True) / stream.shape[1]
             level = lax.rsqrt(mean + 1e-06)
             coarse = level.astype(jnp.bfloat16).astype(jnp.float32)
-            lane = lax.broadcasted_iota(jnp.int32, (ROWS, LANES), 1)
-            extra = share_ref[...].astype(jnp.float32)
+            lane, extra = share_lanes()
             extra = jnp.where(lane == 2 * EXPERTS, coarse, extra)
             extra = jnp.where(lane == 2 * EXPERTS + 1, level - coarse, extra)
             rows_of[chunk][0, :, widths[chunk] :] = extra.astype(jnp.bfloat16)
         for place in range(SPREAD):
             if place:
-                gather_near(chunk, place).start()
+                gather(chunk, place, 0).start()
             if plan.core == 1:
-                gather_across(chunk, place).start()
+                gather(chunk, place, 1).start()
 
     def first_doubling(chunk):
-        when_owning(False, lambda: gather_across(chunk, 0).wait_recv())
-        for place in range(1, SPREAD):
-            gather_near(chunk, place).wait_recv()
-        go(doubling(chunk, halvings - 1))
+        when_owning(True, lambda: arrived(rows_of, pl.ds(1, SPREAD - 1), 1, chunk, NEAR))
+        when_owning(False, lambda: arrived(rows_of, pl.ds(0, SPREAD), 1, chunk, NEAR))
+        doubling(chunk, halvings - 1).start()
 
     def stacked(chunk, columns):
         lines = [
@@ -461,7 +445,7 @@
         elif step <= 2 * halvings + 1:
             done = step - halvings - 2
             doubling(chunk, halvings - done).wait_recv()
-            go(doubling(chunk, halvings - done - 1))
+            doubling(chunk, halvings - done - 1).start()
         else:
             hidden_sums(chunk)
 
@@ -498,26 +482,20 @@
     hidden = hidden / (1.0 + jnp.exp(-hidden)) * (up_sum[base, :] * level)
     act[base, :] = hidden.astype(jnp.bfloat16)
     loads[3].wait()
-    all_sent()
     sum_sent(0)
     staggered(halvings + 2, until_output)
 
     def finish():
-        for code in range(1, GROUP):
-            passing(code).wait_send()
-        for chunk in range(CHUNKS):
-            for place in range(SPREAD):
-                if place:
-                    gather_near(chunk, place).wait_send()
-                if plan.core == 1:
-                    gather_across(chunk, place).wait_send()
+        passed(pl.ds(0, GROUP - 1)).wait_send()
+        near = SPREAD - 1 if plan.core == 0 else 2 * SPREAD - 1
+        sent(rows_of, 1, blocks - SPREAD + near)
 
     def blank():
         out_ref[...] = jnp.zeros_like(out_ref)
+        sent(rows_of, 1, blocks - SPREAD)
 
     when_owning(True, finish)
     when_owning(False, blank)
-    all_sent()
     sum_sent(2)
 
 
@@ -527,7 +505,8 @@
     query_ref,
     residual_ref,
     gain_ref,
-    share_ref,
+    expert_ref,
+    level_ref,
     value_ref,
     cache_hbm,
     out_weight_hbm,
@@ -564,7 +543,7 @@
             ((out_weight_hbm, out_weight), (gate_hbm, gate), (up_hbm, up), (down_hbm, down))
         )
     ]
-    refs = (latent_ref, residual_ref, gain_ref, share_ref, value_ref, out_ref)
+    refs = (latent_ref, residual_ref, gain_ref, expert_ref, level_ref, value_ref, out_ref)
     refs += (out_weight, gate, up, down, latents, left, stream, square, gate_sum, up_sum, act)
     refs += (pass_send, pass_recv, send_sem, recv_sem)
     section = lax.axis_index("sec")
@@ -588,7 +567,7 @@
         )
 
 
-def layer(lengths, queries, residual, gain, shares, value_up, cache, *weights):
+def layer(lengths, queries, residual, gain, experts, levels, value_up, cache, *weights):
     width = residual.shape[1]
     widths = [LANES * units for _, _, units in TABLE]
     hidden = weights[1].shape[1]
@@ -611,10 +590,10 @@
         pltpu.VMEM((GROUP * ROWS, hidden), bf16),
         pltpu.SemaphoreType.DMA((tokens,)),
         pltpu.SemaphoreType.DMA((4,)),
-        pltpu.SemaphoreType.DMA((GROUP,)),
-        pltpu.SemaphoreType.DMA((GROUP,)),
-        pltpu.SemaphoreType.DMA((3, CHUNKS, SLOTS)),
-        pltpu.SemaphoreType.DMA((3, CHUNKS, SLOTS)),
+        pltpu.SemaphoreType.DMA,
+        pltpu.SemaphoreType.DMA,
+        pltpu.SemaphoreType.DMA((2, CHUNKS)),
+        pltpu.SemaphoreType.DMA((2, CHUNKS, SLOTS)),
     ]
     scratch += [pltpu.VMEM((heads * tokens, LANES), f32)] * (latent_width // LANES)
     scratch += [pltpu.VMEM((GROUP, ROWS, w), bf16) for w in widths] * 3
@@ -623,13 +602,13 @@
     return pl.pallas_call(
         functools.partial(layer_kernel, widths),
         out_shape=jax.ShapeDtypeStruct(residual.shape, bf16),
-        in_specs=[pl.BlockSpec(memory_space=pltpu.SMEM)] + [vmem] * 5 + [hbm] * 5,
+        in_specs=[pl.BlockSpec(memory_space=pltpu.SMEM)] + [vmem] * 6 + [hbm] * 5,
         out_specs=vmem,
         scratch_shapes=scratch,
         compiler_params=pltpu.CompilerParams(
             collective_id=0, has_side_effects=True, vmem_limit_bytes=58 * 1024 * 1024
         ),
-    )(lengths, queries, residual, gain, shares, value_up, cache, *weights)
+    )(lengths, queries, residual, gain, experts, levels, value_up, cache, *weights)
 
 
 def body(
@@ -646,19 +625,13 @@
     expert_index,
     gate_level,
 ):
-    levels = gate_level.astype(jnp.float32)
-    mix = levels / jnp.sum(levels, axis=1, keepdims=True)
-    named = expert_index[:, :, None] == jnp.arange(EXPERTS, dtype=jnp.int32)[None, None, :]
-    share = jnp.sum(jnp.where(named, mix[:, :, None], 0.0), axis=1)
-    coarse = share.astype(jnp.bfloat16)
-    fine = (share - coarse.astype(jnp.float32)).astype(jnp.bfloat16)
-    shares = jnp.pad(jnp.concatenate([coarse, fine], axis=1), ((0, 0), (0, 128 - 2 * EXPERTS)))
     return layer(
         cache_length,
         queries,
         residual,
         norm_gain.reshape(1, -1),
-        shares,
+        expert_index.T,
+        gate_level.T,
         value_up,
         jnp.swapaxes(latent_cache, 1, 2),
         out_weight,

time: 101 us -> 92.7 us (0.918)
  Pallas kernels: 96.8 us -> 91 us
  other arithmetic: 2.74 us -> 0 us
    pallas_call x1, Pallas kernels: 96.8 us -> 91 us  [layer(): pl.pallas_call(functools.partial(layer_kernel, widths), out_shape=jax.Sha...]
    reduce_sum x2 -> x0, other arithmetic: 1.39 us -> none  [the longest x1 0.7 us: body(): share = jnp.sum(jnp.where(named, mix[:, :, None], 0.0), axis=1)]
where the time goes in v4:
time: 92.7 us; the launch traced here: 92.6 us
  Pallas kernels  91 us (98%)
  local copies, waits for them, and re-layouts  1.55 us (2%)
    pallas_call x1, Pallas kernels, layer(): pl.pallas_call(functools.partial(layer_kernel, widths), out_shape=jax.Sha...  91 us

profile of v4, /device:TPU:0, one launch (start us, length us, event | category | flops | bytes accessed | tf_op | source)
XLA Modules:
  0.0 92.6 jit_solution(5499156801202595137)
XLA Ops:
  0.0 91.0 %shard_map.118 = bf16[8,7168]{1,0:T(8,128)(2,1)} custom-call(s32[8]{0:T(128)} %length_ref.1, bf16[8,64,576]{2,1,0:T(8,128)(2,1)} %query_ref.1, bf16[8,7168]{1,0:T(8,128)(2,1)} %residual_ref.1, f32[1,7168]{1,0:T(1,128)} %bitcast.5, s32[2,8]{1,0:T(2,128)} %bitcast.6, s32[2,8]{1,0:T(2,128)} %bitcast.7, bf16[2,512,128]{2,1,0:T(8,128)(2,1)} %value_ref.1, ...), custom_call_target="tpu_custom_call" | custom-call | tf_op jit(solution)/shard_map/pallas_call | solution.py:602
  91.0 1.6 %copy.14 = bf16[8,7168]{1,0:T(8,128)(2,1)} copy(bf16[8,7168]{1,0:T(8,128)(2,1)} %shard_map.118) | data formatting | bytes 229376

commit v5 on v4

--- a/solution.py
+++ b/solution.py
@@ -15,16 +15,26 @@
 TILE = 256
 LANES = 128
 TABLE = (
-    ((0, 1, 2, 3, 4), 0, 6),
-    ((1, 2, 3, 4, 0), 1, 6),
-    ((2, 3, 4, 0, 1), 2, 6),
-    ((3, 4, 0, 1, 2), 3, 6),
-    ((4, 0, 1, 2, 3), 0, 6),
-    ((0, 1, 2, 3, 4), 2, 6),
-    ((1, 2, 3, 4, 0), 3, 5),
-    ((2, 3, 4, 0, 1), 0, 5),
-    ((3, 4, 0, 1, 2), 1, 5),
-    ((4, 0, 1, 2, 3), 1, 5),
+    ((0, 1, 2, 3, 4), 0, 3),
+    ((1, 2, 3, 4, 0), 1, 3),
+    ((2, 3, 4, 0, 1), 2, 3),
+    ((3, 4, 0, 1, 2), 3, 3),
+    ((4, 0, 1, 2, 3), 0, 3),
+    ((0, 1, 2, 3, 4), 1, 3),
+    ((1, 2, 3, 4, 0), 2, 3),
+    ((2, 3, 4, 0, 1), 3, 3),
+    ((3, 4, 0, 1, 2), 0, 3),
+    ((4, 0, 1, 2, 3), 1, 3),
+    ((0, 1, 2, 3, 4), 2, 3),
+    ((1, 2, 3, 4, 0), 3, 3),
+    ((2, 3, 4, 0, 1), 0, 3),
+    ((3, 4, 0, 1, 2), 1, 3),
+    ((4, 0, 1, 2, 3), 2, 3),
+    ((0, 1, 2, 3, 4), 3, 3),
+    ((1, 2, 3, 4, 0), 0, 2),
+    ((2, 3, 4, 0, 1), 1, 2),
+    ((3, 4, 0, 1, 2), 2, 2),
+    ((4, 0, 1, 2, 3), 3, 2),
 )
 LAG = 0
 CHUNKS = len(TABLE)

time: 92.7 us -> 87.1 us (0.940)
  Pallas kernels: 91 us -> 85.4 us
    pallas_call x1, Pallas kernels: 91 us -> 85.4 us  [layer(): pl.pallas_call(functools.partial(layer_kernel, widths), out_shape=jax.Sha...]
where the time goes in v5:
time: 87.1 us; the launch traced here: 87 us
  Pallas kernels  85.4 us (98%)
  local copies, waits for them, and re-layouts  1.55 us (2%)
    pallas_call x1, Pallas kernels, layer(): pl.pallas_call(functools.partial(layer_kernel, widths), out_shape=jax.Sha...  85.4 us

profile of v5, /device:TPU:0, one launch (start us, length us, event | category | flops | bytes accessed | tf_op | source)
XLA Modules:
  0.0 87.0 jit_solution(5312727255754291392)
XLA Ops:
  0.0 85.4 %shard_map.118 = bf16[8,7168]{1,0:T(8,128)(2,1)} custom-call(s32[8]{0:T(128)} %length_ref.1, bf16[8,64,576]{2,1,0:T(8,128)(2,1)} %query_ref.1, bf16[8,7168]{1,0:T(8,128)(2,1)} %residual_ref.1, f32[1,7168]{1,0:T(1,128)} %bitcast.5, s32[2,8]{1,0:T(2,128)} %bitcast.6, s32[2,8]{1,0:T(2,128)} %bitcast.7, bf16[2,512,128]{2,1,0:T(8,128)(2,1)} %value_ref.1, ...), custom_call_target="tpu_custom_call" | custom-call | tf_op jit(solution)/shard_map/pallas_call | solution.py:612
  85.4 1.6 %copy.14 = bf16[8,7168]{1,0:T(8,128)(2,1)} copy(bf16[8,7168]{1,0:T(8,128)(2,1)} %shard_map.118) | data formatting | bytes 229376

commit v6 on v5

--- a/solution.py
+++ b/solution.py
@@ -12,7 +12,6 @@
 ROWS = 8
 GROUP = 32
 DIMS = 5
-TILE = 256
 LANES = 128
 TABLE = (
     ((0, 1, 2, 3, 4), 0, 3),
@@ -39,8 +38,8 @@
 LAG = 0
 CHUNKS = len(TABLE)
 SPREAD = 4
-NEAR, FAR, HALVED = 0, 1, 2
-SLOTS = HALVED + 3
+NEAR, HALVED, FAR = 0, 1, 3
+SLOTS = 4
 MASKS = (1, 2, 6, 8, 24)
 MESH = pl.DeviceIdType.MESH
 
@@ -115,16 +114,29 @@
         )
 
 
-def attend(query_ref, length_ref, cache_hbm, cache, by_head, latent_ref, cache_sem, start_loads):
+def attend(
+    query_hbm,
+    query_ref,
+    length_ref,
+    cache_hbm,
+    cache,
+    by_head,
+    latent_ref,
+    cache_sem,
+    start_loads,
+):
     tokens, heads, _ = query_ref.shape
     latent_width = LANES * len(by_head)
     value_width = LANES
     score_scale = (value_width + query_ref.shape[2] - latent_width) ** (-0.5)
+    query_fetch = pltpu.make_async_copy(query_hbm, query_ref, cache_sem.at[tokens])
+    query_fetch.start()
     fetches = []
     for token in range(tokens):
         fetch = pltpu.make_async_copy(cache_hbm.at[token], cache.at[token], cache_sem.at[token])
         fetch.start()
         fetches.append(fetch)
+    query_fetch.wait()
     position = lax.broadcasted_iota(jnp.int32, (heads, cache.shape[2]), 1)
     for token in range(tokens):
         fetches[token].wait()
@@ -226,6 +238,7 @@
 
     when_owning(True, pass_out)
     when_owning(False, lambda: passed(pl.ds(0, blocks)).wait_recv())
+    loads[0].wait()
     for head in range(2):
         lines = latents[pl.ds(0, blocks), head * ROWS : (head + 1) * ROWS, :].astype(jnp.float32)
         lines = lines.reshape(rows, lines.shape[2]).astype(jnp.bfloat16)
@@ -323,30 +336,14 @@
                 total = total + landings[phase][chunk][16 + place].astype(jnp.float32)
         return total
 
-    def tiled(chunk, one):
-        whole = widths[chunk] // TILE
-
-        @pl.loop(0, whole)
-        def _(i):
-            one(pl.multiple_of(i * TILE, TILE), TILE)
-
-        if widths[chunk] % TILE:
-            one(whole * TILE, widths[chunk] % TILE)
-
     def project(chunk, operand, weight, scale):
-        def one(offset, size):
-            inner = pl.ds(offset, size)
-            outer = pl.ds(pl.multiple_of(starts[chunk] + offset, LANES), size)
-            product = jnp.dot(
-                operand[base, :], weight[:, outer], preferred_element_type=jnp.float32
-            )
-            if scale is not None:
-                product = product * scale
-            for i, code in enumerate(plan.codes()):
-                block = product[i * ROWS : (i + 1) * ROWS]
-                partial[chunk][plan.place(chunk, code), :, inner] = block.astype(jnp.bfloat16)
-
-        tiled(chunk, one)
+        columns = pl.ds(starts[chunk], widths[chunk])
+        product = jnp.dot(operand[base, :], weight[:, columns], preferred_element_type=jnp.float32)
+        if scale is not None:
+            product = product * scale
+        for i, code in enumerate(plan.codes()):
+            block = product[i * ROWS : (i + 1) * ROWS]
+            partial[chunk][plan.place(chunk, code)] = block.astype(jnp.bfloat16)
 
     def gather(chunk, place, across):
         return copy_of(
@@ -427,13 +424,10 @@
     def hidden_sums(chunk):
         doubling(chunk, 0).wait_recv()
 
-        def one(offset, size):
-            outer = pl.ds(pl.multiple_of(starts[chunk] + offset, LANES), size)
-            lines = stacked(chunk, pl.ds(offset, size)).astype(jnp.bfloat16)
-            gate_sum[base, :] += jnp.dot(lines, gate[outer, :], preferred_element_type=jnp.float32)
-            up_sum[base, :] += jnp.dot(lines, up[outer, :], preferred_element_type=jnp.float32)
-
-        tiled(chunk, one)
+        columns = pl.ds(starts[chunk], widths[chunk])
+        lines = stacked(chunk, pl.ds(0, widths[chunk])).astype(jnp.bfloat16)
+        gate_sum[base, :] += jnp.dot(lines, gate[columns, :], preferred_element_type=jnp.float32)
+        up_sum[base, :] += jnp.dot(lines, up[columns, :], preferred_element_type=jnp.float32)
 
     def staggered(count, stage):
         for time in range(count + LAG * (CHUNKS // DIMS - 1)):
@@ -475,7 +469,7 @@
 
     gate_sum[base, :] = jnp.zeros((rows, gate_sum.shape[1]), jnp.float32)
     up_sum[base, :] = jnp.zeros((rows, up_sum.shape[1]), jnp.float32)
-    for load in loads[:3]:
+    for load in loads[1:6]:
         load.wait()
     staggered(2 * halvings + 3, until_hidden)
     shares = stacked(CHUNKS - 1, pl.ds(widths[CHUNKS - 1], LANES))
@@ -491,7 +485,7 @@
     hidden = gate_sum[base, :] * level
     hidden = hidden / (1.0 + jnp.exp(-hidden)) * (up_sum[base, :] * level)
     act[base, :] = hidden.astype(jnp.bfloat16)
-    loads[3].wait()
+    loads[6].wait()
     sum_sent(0)
     staggered(halvings + 2, until_output)
 
@@ -512,23 +506,27 @@
 def layer_kernel(
     widths,
     length_ref,
-    query_ref,
-    residual_ref,
-    gain_ref,
     expert_ref,
     level_ref,
-    value_ref,
+    query_hbm,
     cache_hbm,
+    value_hbm,
+    residual_hbm,
+    gain_hbm,
     out_weight_hbm,
     gate_hbm,
     up_hbm,
     down_hbm,
     out_ref,
+    query_ref,
+    cache,
+    value_ref,
+    residual_ref,
+    gain_ref,
     out_weight,
     gate,
     up,
     down,
-    cache,
     latent_ref,
     latents,
     left,
@@ -550,7 +548,15 @@
     loads = [
         pltpu.make_async_copy(source, target, load_sem.at[i])
         for i, (source, target) in enumerate(
-            ((out_weight_hbm, out_weight), (gate_hbm, gate), (up_hbm, up), (down_hbm, down))
+            (
+                (value_hbm, value_ref),
+                (residual_hbm, residual_ref),
+                (gain_hbm, gain_ref),
+                (out_weight_hbm, out_weight),
+                (gate_hbm, gate),
+                (up_hbm, up),
+                (down_hbm, down),
+            )
         )
     ]
     refs = (latent_ref, residual_ref, gain_ref, expert_ref, level_ref, value_ref, out_ref)
@@ -567,7 +573,15 @@
 
     pl.when(section < 3)(
         lambda: attend(
-            query_ref, length_ref, cache_hbm, cache, by_head, latent_ref, cache_sem, start_loads
+            query_hbm,
+            query_ref,
+            length_ref,
+            cache_hbm,
+            cache,
+            by_head,
+            latent_ref,
+            cache_sem,
+            start_loads,
         )
     )
     pl.when(section == 3)(start_loads)
@@ -577,19 +591,19 @@
         )
 
 
-def layer(lengths, queries, residual, gain, experts, levels, value_up, cache, *weights):
+def layer(lengths, experts, levels, queries, cache, *weights):
+    value_up, residual = weights[:2]
     width = residual.shape[1]
     widths = [LANES * units for _, _, units in TABLE]
-    hidden = weights[1].shape[1]
+    hidden = weights[4].shape[1]
     tokens, heads, _ = queries.shape
     latent_width = value_up.shape[1]
     bf16, f32 = jnp.bfloat16, jnp.float32
     vmem = pl.BlockSpec(memory_space=pltpu.VMEM)
     hbm = pl.BlockSpec(memory_space=pl.ANY)
     latents = pltpu.VMEM((GROUP, heads * tokens // GROUP, latent_width), bf16)
-    scratch = [pltpu.VMEM(weight.shape, bf16) for weight in weights]
+    scratch = [pltpu.VMEM(array.shape, array.dtype) for array in (queries, cache, *weights)]
     scratch += [
-        pltpu.VMEM(cache.shape, bf16),
         latents,
         latents,
         pltpu.VMEM((GROUP * ROWS, 2 * LANES), bf16),
@@ -598,8 +612,8 @@
         pltpu.VMEM((GROUP * ROWS, hidden), f32),
         pltpu.VMEM((GROUP * ROWS, hidden), f32),
         pltpu.VMEM((GROUP * ROWS, hidden), bf16),
-        pltpu.SemaphoreType.DMA((tokens,)),
-        pltpu.SemaphoreType.DMA((4,)),
+        pltpu.SemaphoreType.DMA((tokens + 1,)),
+        pltpu.SemaphoreType.DMA((len(weights),)),
         pltpu.SemaphoreType.DMA,
         pltpu.SemaphoreType.DMA,
         pltpu.SemaphoreType.DMA((2, CHUNKS)),
@@ -612,13 +626,13 @@
     return pl.pallas_call(
         functools.partial(layer_kernel, widths),
         out_shape=jax.ShapeDtypeStruct(residual.shape, bf16),
-        in_specs=[pl.BlockSpec(memory_space=pltpu.SMEM)] + [vmem] * 6 + [hbm] * 5,
+        in_specs=[pl.BlockSpec(memory_space=pltpu.SMEM)] + [vmem] * 2 + [hbm] * 9,
         out_specs=vmem,
         scratch_shapes=scratch,
         compiler_params=pltpu.CompilerParams(
             collective_id=0, has_side_effects=True, vmem_limit_bytes=58 * 1024 * 1024
         ),
-    )(lengths, queries, residual, gain, experts, levels, value_up, cache, *weights)
+    )(lengths, experts, levels, queries, cache, *weights)
 
 
 def body(
@@ -637,13 +651,13 @@
 ):
     return layer(
         cache_length,
+        expert_index.T,
+        gate_level.T,
         queries,
+        jnp.swapaxes(latent_cache, 1, 2),
+        value_up,
         residual,
         norm_gain.reshape(1, -1),
-        expert_index.T,
-        gate_level.T,
-        value_up,
-        jnp.swapaxes(latent_cache, 1, 2),
         out_weight,
         gate_weight,
         up_weight,

time: 87.1 us -> 86.4 us (level)
  no operation moved by 1% of the time
where the time goes in v6:
time: 86.4 us; the launch traced here: 86.3 us
  Pallas kernels  84.7 us (98%)
  local copies, waits for them, and re-layouts  1.55 us (2%)
    pallas_call x1, Pallas kernels, layer(): pl.pallas_call(functools.partial(layer_kernel, widths), out_shape=jax.Sha...  84.7 us

profile of v6, /device:TPU:0, one launch (start us, length us, event | category | flops | bytes accessed | tf_op | source)
XLA Modules:
  0.0 86.3 jit_solution(2414403251695096895)
XLA Ops:
  0.0 84.7 %shard_map.118 = bf16[8,7168]{1,0:T(8,128)(2,1)} custom-call(s32[8]{0:T(128)} %length_ref.1, s32[2,8]{1,0:T(2,128)} %bitcast.6, s32[2,8]{1,0:T(2,128)} %bitcast.7, bf16[8,64,576]{2,1,0:T(8,128)(2,1)} %query_hbm.1, bf16[8,576,1024]{2,1,0:T(8,128)(2,1)} %bitcast.4, bf16[2,512,128]{2,1,0:T(8,128)(2,1)} %value_hbm.1, bf16[8,7168]{1,0:T(8,128)(2,1)} %residual_hbm.1, ...), custom_call_target="tpu_custom_call" | custom-call | tf_op jit(solution)/shard_map/pallas_call | solution.py:626
  84.7 1.6 %copy.14 = bf16[8,7168]{1,0:T(8,128)(2,1)} copy(bf16[8,7168]{1,0:T(8,128)(2,1)} %shard_map.118) | data formatting | bytes 229376
